TPU v7x, 32 devices: a whole 2x2x4 slice. The times are simulated.
32 devices in a mesh: dp: 8 (over z, x), mp: 4 (over y, core).
Axes of the slice: x: 2, y: 2, z: 4, core: 2. Of those that a mesh axis runs over, the one named last changes fastest.
Arguments:
- tokens: bfloat16 [32768, 768], P(('dp', 'mp')), may hold values from -6 to 6
- w_qkv: bfloat16 [768, 2304], replicated, may hold values from -0.21875 to 0.21875
- bias_q: bfloat16 [768], replicated, may hold values from -3 to 3
- bias_v: bfloat16 [768], replicated, may hold values from -3 to 3
- w_out: bfloat16 [768, 768], replicated, may hold values from -0.4375 to 0.4375
- bias_out: bfloat16 [768], replicated, may hold values from -3 to 3
- norm1_gain: bfloat16 [768], replicated, may hold values from 0.5 to 1.5
- norm1_bias: bfloat16 [768], replicated, may hold values from -2 to 2
- w_in: bfloat16 [3072, 768], P('mp'), may hold values from -0.21875 to 0.21875
- bias_in: bfloat16 [3072], P('mp'), may hold values from -3 to 3
- w_down: bfloat16 [3072, 768], P('mp'), may hold values from -0.109375 to 0.109375
- bias_down: bfloat16 [768], replicated, may hold values from -3 to 3
- norm2_gain: bfloat16 [768], replicated, may hold values from 0.5 to 1.5
- norm2_bias: bfloat16 [768], replicated, may hold values from -2 to 2
- mask_logits: float32 [12, 512, 512], P(None, ('dp', 'mp')), may hold values from -8 to 8
- mask_noise: int32 [12, 512, 512], P(None, ('dp', 'mp')), may hold values from 1 to 65535
- grad_out: bfloat16 [32768, 768], P(('dp', 'mp')), may hold values from -6 to 6
Outputs:
- out: bfloat16 [32768, 768], P(('dp', 'mp'))
- grad_tokens: bfloat16 [32768, 768], P(('dp', 'mp'))
- grad_w_qkv: float32 [768, 2304], replicated
- grad_bias_q: float32 [768], replicated
- grad_bias_v: float32 [768], replicated
- grad_w_out: float32 [768, 768], replicated
- grad_bias_out: float32 [768], replicated
- grad_norm1_gain: float32 [768], replicated
- grad_norm1_bias: float32 [768], replicated
- grad_w_in: float32 [3072, 768], P('mp')
- grad_bias_in: float32 [3072], P('mp')
- grad_w_down: float32 [3072, 768], P('mp')
- grad_bias_down: float32 [768], replicated
- grad_norm2_gain: float32 [768], replicated
- grad_norm2_bias: float32 [768], replicated
- grad_mask_logits: float32 [12, 512, 512], P(None, ('dp', 'mp'))
All inputs are finite; a program needn't handle non-finite values.
Results may differ from a plain program's by a relative error of at most 0.013.
The roundings to bfloat16 on the way count: a program that leaves them out, or rounds other values in their place, can miss the bound.
Values may be sent and summed in bfloat16 or wider, within the bound.
No kernel may reach another device: no remote copies, remote signals or barrier semaphores. Data moves between devices by JAX's collectives and lax.ppermute only.
A program may use at most 256 MiB of HBM per device.

v0:
```python
import math

import jax
import jax.numpy as jnp
from jax import lax
from jax.sharding import PartitionSpec as P

MASK_SCALE = 4.0
NORM_EPS = 1e-12
CONTRACT_LAST = (((1,), (1,)), ((), ()))
CONTRACT_FIRST = (((0,), (0,)), ((), ()))
SQRT_HALF = 0.7071067811865476
INV_ROOT_TWO_PI = 0.3989422804014327


def norm_forward(value, gain, shift):
    center = jnp.mean(value, axis=-1, keepdims=True)
    centered = value - center
    inverse = lax.rsqrt(jnp.mean(centered * centered, axis=-1, keepdims=True) + NORM_EPS)
    normal = centered * inverse
    return (normal * gain + shift, normal, inverse)


def norm_backward(grad, normal, inverse, gain):
    inner = grad * gain
    back = inverse * (
        inner
        - jnp.mean(inner, axis=-1, keepdims=True)
        - normal * jnp.mean(inner * normal, axis=-1, keepdims=True)
    )
    return (back, jnp.sum(grad * normal, axis=0), jnp.sum(grad, axis=0))


def gelu_slope(value):
    return (
        0.5 * (1.0 + lax.erf(value * SQRT_HALF))
        + value * jnp.exp(-0.5 * value * value) * INV_ROOT_TWO_PI
    )


def body(
    tokens,
    w_qkv,
    bias_q,
    bias_v,
    w_out,
    bias_out,
    norm1_gain,
    norm1_bias,
    w_in,
    bias_in,
    w_down,
    bias_down,
    norm2_gain,
    norm2_bias,
    mask_logits,
    mask_noise,
    grad_out,
):
    width = w_out.shape[0]
    heads = mask_logits.shape[0]
    length = mask_logits.shape[2]
    head_size = width // heads
    factor = 1.0 / math.sqrt(head_size)
    count = tokens.shape[0] // length
    own_rows = tokens.shape[0]
    fraction = mask_noise.astype(jnp.float32) / 65536.0
    mask_own = jax.nn.sigmoid(mask_logits + jnp.log(fraction) - jnp.log(1.0 - fraction))
    mask_all = lax.all_gather(mask_own, ("dp", "mp"), axis=1, tiled=True)
    mask_bias = MASK_SCALE * (mask_all - 1.0)
    shift_qkv = jnp.concatenate(
        [bias_q.astype(jnp.float32), jnp.zeros((width,), jnp.float32), bias_v.astype(jnp.float32)]
    )
    projected = (jnp.dot(tokens, w_qkv, preferred_element_type=jnp.float32) + shift_qkv).astype(
        jnp.bfloat16
    )
    split = projected.reshape(count, length, 3, heads, head_size)

    def forward_one(sequence):
        scores = (
            jnp.einsum(
                "qhd,khd->hqk", sequence[:, 0], sequence[:, 1], preferred_element_type=jnp.float32
            )
            * factor
            + mask_bias
        )
        highest = jnp.max(scores, axis=-1, keepdims=True)
        powers = jnp.exp(scores - highest)
        summed = jnp.sum(powers, axis=-1, keepdims=True)
        probs = (powers / summed).astype(jnp.bfloat16)
        mixed = jnp.einsum(
            "hqk,khd->qhd", probs, sequence[:, 2], preferred_element_type=jnp.float32
        )
        return (
            mixed.reshape(length, width).astype(jnp.bfloat16),
            highest[..., 0] + jnp.log(summed[..., 0]),
        )

    mixed, log_total = lax.map(forward_one, split)
    mixed = mixed.reshape(own_rows, width)
    attn = jnp.dot(mixed, w_out, preferred_element_type=jnp.float32) + bias_out.astype(jnp.float32)
    gain_one = norm1_gain.astype(jnp.float32)
    first, normal_one, inverse_one = norm_forward(
        tokens.astype(jnp.float32) + attn, gain_one, norm1_bias.astype(jnp.float32)
    )
    first_low = first.astype(jnp.bfloat16)
    full_in, full_bias, full_down = (w_in, bias_in, w_down)
    ffn_inputs = lax.all_gather(first_low, "mp", axis=0, tiled=True)
    pre = lax.dot_general(
        ffn_inputs, full_in, CONTRACT_LAST, preferred_element_type=jnp.float32
    ) + full_bias.astype(jnp.float32)
    active = jax.nn.gelu(pre, approximate=False).astype(jnp.bfloat16)
    branch = lax.psum_scatter(
        jnp.dot(active, w_down, preferred_element_type=jnp.float32),
        "mp",
        scatter_dimension=0,
        tiled=True,
    )
    gain_two = norm2_gain.astype(jnp.float32)
    result, normal_two, inverse_two = norm_forward(
        first + branch + bias_down.astype(jnp.float32), gain_two, norm2_bias.astype(jnp.float32)
    )
    grad_second, grad_gain_two, grad_shift_two = norm_backward(
        grad_out.astype(jnp.float32), normal_two, inverse_two, gain_two
    )
    grad_bias_down = jnp.sum(grad_second, axis=0)
    grad_branch = grad_second.astype(jnp.bfloat16)
    grad_rows = lax.all_gather(grad_branch, "mp", axis=0, tiled=True)
    grad_active = lax.dot_general(
        grad_rows, full_down, CONTRACT_LAST, preferred_element_type=jnp.float32
    )
    grad_pre = (grad_active * gelu_slope(pre)).astype(jnp.bfloat16)
    part_down = lax.dot_general(
        active, grad_rows, CONTRACT_FIRST, preferred_element_type=jnp.float32
    )
    part_in = lax.dot_general(
        grad_pre, ffn_inputs, CONTRACT_FIRST, preferred_element_type=jnp.float32
    )
    part_bias = jnp.sum(grad_pre.astype(jnp.float32), axis=0)
    grad_first_ffn = lax.psum_scatter(
        jnp.dot(grad_pre, w_in, preferred_element_type=jnp.float32),
        "mp",
        scatter_dimension=0,
        tiled=True,
    )
    grad_w_in, grad_bias_in, grad_w_down = lax.psum((part_in, part_bias, part_down), "dp")
    grad_one, grad_gain_one, grad_shift_one = norm_backward(
        grad_second + grad_first_ffn, normal_one, inverse_one, gain_one
    )
    grad_bias_out = jnp.sum(grad_one, axis=0)
    grad_attn = grad_one.astype(jnp.bfloat16)
    grad_w_out = lax.dot_general(
        mixed, grad_attn, CONTRACT_FIRST, preferred_element_type=jnp.float32
    )
    grad_mixed = lax.dot_general(
        grad_attn, w_out, CONTRACT_LAST, preferred_element_type=jnp.float32
    ).astype(jnp.bfloat16)
    grad_split = grad_mixed.reshape(count, length, heads, head_size)

    def backward_one(carry, item):
        sequence, grad_sequence, log_sequence = item
        query = sequence[:, 0]
        keys = sequence[:, 1]
        values = sequence[:, 2]
        scores = (
            jnp.einsum("qhd,khd->hqk", query, keys, preferred_element_type=jnp.float32) * factor
            + mask_bias
        )
        probs = jnp.exp(scores - log_sequence[..., None])
        grad_probs = jnp.einsum(
            "qhd,khd->hqk", grad_sequence, values, preferred_element_type=jnp.float32
        )
        grad_values = jnp.einsum(
            "hqk,qhd->khd",
            probs.astype(jnp.bfloat16),
            grad_sequence,
            preferred_element_type=jnp.float32,
        )
        inner = jnp.sum(probs * grad_probs, axis=-1, keepdims=True)
        grad_scores = probs * (grad_probs - inner)
        grad_low = grad_scores.astype(jnp.bfloat16)
        grad_query = (
            jnp.einsum("hqk,khd->qhd", grad_low, keys, preferred_element_type=jnp.float32) * factor
        )
        grad_keys = (
            jnp.einsum("hqk,qhd->khd", grad_low, query, preferred_element_type=jnp.float32) * factor
        )
        stacked = jnp.stack([grad_query, grad_keys, grad_values], axis=1).astype(jnp.bfloat16)
        return (carry + grad_scores, stacked)

    mask_term, grad_qkv = lax.scan(
        backward_one,
        jnp.zeros((heads, length, length), jnp.float32),
        (split, grad_split, log_total),
    )
    grad_qkv = grad_qkv.reshape(own_rows, 3 * width)
    grad_mask_own = lax.psum_scatter(
        MASK_SCALE * mask_term, ("dp", "mp"), scatter_dimension=1, tiled=True
    )
    grad_mask_logits = grad_mask_own * mask_own * (1.0 - mask_own)
    grad_w_qkv = lax.dot_general(
        tokens, grad_qkv, CONTRACT_FIRST, preferred_element_type=jnp.float32
    )
    grad_wide = grad_qkv.astype(jnp.float32)
    grad_bias_q = jnp.sum(grad_wide[:, :width], axis=0)
    grad_bias_v = jnp.sum(grad_wide[:, 2 * width :], axis=0)
    grad_tokens = (
        grad_one
        + lax.dot_general(grad_qkv, w_qkv, CONTRACT_LAST, preferred_element_type=jnp.float32)
    ).astype(jnp.bfloat16)
    (
        grad_w_qkv,
        grad_w_out,
        grad_bias_q,
        grad_bias_v,
        grad_bias_out,
        grad_gain_one,
        grad_shift_one,
        grad_bias_down,
        grad_gain_two,
        grad_shift_two,
    ) = lax.psum(
        (
            grad_w_qkv,
            grad_w_out,
            grad_bias_q,
            grad_bias_v,
            grad_bias_out,
            grad_gain_one,
            grad_shift_one,
            grad_bias_down,
            grad_gain_two,
            grad_shift_two,
        ),
        ("dp", "mp"),
    )
    return (
        result.astype(jnp.bfloat16),
        grad_tokens,
        grad_w_qkv,
        grad_bias_q,
        grad_bias_v,
        grad_w_out,
        grad_bias_out,
        grad_gain_one,
        grad_shift_one,
        grad_w_in,
        grad_bias_in,
        grad_w_down,
        grad_bias_down,
        grad_gain_two,
        grad_shift_two,
        grad_mask_logits,
    )


def solution(mesh):
    return jax.shard_map(
        body,
        mesh=mesh,
        in_specs=(
            P(("dp", "mp"), None),
            P(),
            P(),
            P(),
            P(),
            P(),
            P(),
            P(),
            P("mp", None),
            P("mp"),
            P("mp", None),
            P(),
            P(),
            P(),
            P(None, ("dp", "mp"), None),
            P(None, ("dp", "mp"), None),
            P(("dp", "mp"), None),
        ),
        out_specs=(
            P(("dp", "mp"), None),
            P(("dp", "mp"), None),
            P(),
            P(),
            P(),
            P(),
            P(),
            P(),
            P(),
            P("mp", None),
            P("mp"),
            P("mp", None),
            P(),
            P(),
            P(),
            P(None, ("dp", "mp"), None),
        ),
        check_vma=False,
    )
```

profile of v0, /device:TPU:0, one launch (start us, length us, event | category | flops | bytes accessed | tf_op | source)
XLA Modules:
  0.0 1236.1 jit_solution(10080899975197393362)
XLA Ops:
  43.7 66.6 %all-gather.4.cloned.1.call-done = f32[12,512,512]{2,1,0:T(8,128)} async-done(((f32[12,16,512]{2,1,0:T(8,128)}), f32[12,512,512]{2,1,0:T(8,128)}) %all-gather.4.cloned.1.call-update) | async-done | bytes 12582928 | tf_op jit(solution)/shard_map/all_gather | solution.py:69
  110.3 10.6 add_multiply_fusion
  121.0 12.6 %copy.58 = f32[12,512,512]{1,2,0:T(8,128)} copy(f32[12,512,512]{2,1,0:T(8,128)} %add_multiply_fusion) | data formatting | bytes 25165824 | tf_op jit(solution)/shard_map/while | solution.py:99
  133.6 38.1 %while.25 = (s32[]{:T(128)}, bf16[2,512,768]{2,1,0:T(8,128)(2,1)}, f32[2,12,512]{2,1,0:T(8,128)}, bf16[2,512,3,12,64]{1,4,3,2,0:T(8,128)(2,1)}, f32[12,512,512]{1,2,0:T(8,128)}, /*index=5*/s32[]{:T(128)}) while((s32[]{:T(128)}, bf16[2,512,768]{2,1,0:T(8,128)(2,1)}, f32[2,12,512]{2,1,0:T(8,128)}, bf16[2,512,3,12,64]{1,4,3,2,0:T(8,128)(2,1)}, ...), condition=%wide.region_3.4_spmd, body=%wide.region_0.3_spmd.sunk | while | flops 830859264 | bytes 71393952 | solution.py:99
  180.3 43.8 %all-gather.6.cloned.1.call-done = bf16[4096,768]{0,1:T(8,128)(2,1)} async-done(((bf16[1024,768]{0,1:T(8,128)(2,1)}), bf16[4096,768]{0,1:T(8,128)(2,1)}) %all-gather.6.cloned.1.call-update) | async-done | bytes 6291472 | tf_op jit(solution)/shard_map/all_gather | solution.py:108
  224.1 35.5 %fusion.23 = (bf16[4096,768]{1,0:T(8,128)(2,1)S(1)}, f32[4096,768]{1,0:T(8,128)}) fusion(f32[768]{0:T(1024)} %convert_element_type.111, bf16[4096,768]{0,1:T(8,128)(2,1)} %all-gather.6.cloned.1.call-done, bf16[768,768]{1,0:T(8,128)(2,1)} %param.29), kind=kOutput, calls=%fused_computation.42 | convolution fusion | flops 5039456256 | bytes 26348544 | tf_op jit(solution)/shard_map/dot_general | solution.py:109
  275.6 93.8 %reduce-scatter.4.cloned.1.call-done = f32[1024,768]{0,1:T(8,128)} async-done(((f32[4096,768]{0,1:T(8,128)}), f32[1024,768]{0,1:T(8,128)}) %reduce-scatter.4.cloned.1.call-update) | async-done | bytes 3145744 | tf_op jit(solution)/shard_map/reduce_scatter | solution.py:113
  377.1 46.5 %all-gather.8.cloned.1.call-done = bf16[4096,768]{0,1:T(8,128)(2,1)} async-done(((bf16[1024,768]{0,1:T(8,128)(2,1)}), bf16[4096,768]{0,1:T(8,128)(2,1)}) %all-gather.8.cloned.1.call-update) | async-done | bytes 6291472 | tf_op jit(solution)/shard_map/all_gather | solution.py:128
  423.6 13.1 %convert_reduce_fusion = (f32[768]{0:T(1024)}, bf16[4096,768]{1,0:T(8,128)(2,1)S(1)}) fusion(f32[4096,768]{1,0:T(8,128)} %get-tuple-element.233, f32[768]{0:T(1024)} %convert_element_type.111, bf16[4096,768]{0,1:T(8,128)(2,1)} %all-gather.8.cloned.1.call-done, bf16[768,768]{1,0:T(8,128)(2,1)} %param.31), kind=kOutput, calls=%fused_computation.49 | convolution fusion | flops 4872731648 | bytes 26351616 | tf_op jit(solution)/shard_map/dot_general | solution.py:129
  448.7 97.9 %reduce-scatter.6.cloned.1.call-done = f32[1024,768]{0,1:T(8,128)} async-done(((f32[4096,768]{0,1:T(8,128)}), f32[1024,768]{0,1:T(8,128)}) %reduce-scatter.6.cloned.1.call-update) | async-done | bytes 3145744 | tf_op jit(solution)/shard_map/reduce_scatter | solution.py:140
  571.5 100.8 %while.26 = (s32[]{:T(128)}, f32[12,512,512]{1,2,0:T(8,128)}, bf16[2,512,3,12,64]{1,4,3,2,0:T(8,128)(2,1)}, bf16[2,512,3,12,64]{1,4,3,2,0:T(8,128)(2,1)}, f32[12...) while((s32[]{:T(128)}, f32[12,512,512]{1,2,0:T(8,128)}, ...), condition=%wide.region_16.17_spmd.clone, body=%wide.region_14.16_spmd.clone.sunk | while | flops 2056906752 | bytes 225248528 | solution.py:191
  580.2 14.8 %multiply_reduce_fusion.7 = (f32[12,512]{1,0:T(8,128)}, f32[12,512,512]{1,2,0:T(8,128)}) fusion(f32[12,512,512]{1,2,0:T(8,128)} %fusion.105, f32[12,512]{1,0:T(8,128)S(1)} %dynamic-slice_bitcast_fusion.8, f32[12,512,512]{1,2,0:T(8,128)} %get-tuple-element.364, bf16[512,3,12,64]{0,3,2,1:T(8,128)(2,1)S(1)} %dynamic-slice_bitcast_fusion.7), kind=kOutput, calls=%fused_computation.14.clone.1 | convolution fusion | flops 418375680 | bytes 39378944 | tf_op jit(solution)/shard_map/while/body/eval_jaxpr/qhd,khd->hqk/dot_general | solution.py:166
  595.0 16.0 %fusion.106 = (bf16[12,512,512]{1,2,0:T(8,128)(2,1)S(1)}, f32[12,512,512]{1,2,0:T(8,128)}) fusion(f32[12,512,512]{1,2,0:T(8,128)} %get-tuple-element.320, f32[12,512,512]{1,2,0:T(8,128)} %fusion.105, f32[12,512]{1,0:T(8,128)} %get-tuple-element.321, f32[12,512,512]{1,2,0:T(8,128)} %get-tuple-element.352, pred[]{:T(512)S(6)} %compare.3), kind=kLoop, calls=%fused_computation.18.clone.1 | loop fusion | flops 15728640 | bytes 56647680 | tf_op jit(solution)/shard_map/while/body/eval_jaxpr/convert_element_type | solution.py:181
  628.9 14.8 %multiply_reduce_fusion.7 = (f32[12,512]{1,0:T(8,128)}, f32[12,512,512]{1,2,0:T(8,128)}) fusion(f32[12,512,512]{1,2,0:T(8,128)} %fusion.105, f32[12,512]{1,0:T(8,128)S(1)} %dynamic-slice_bitcast_fusion.8, f32[12,512,512]{1,2,0:T(8,128)} %get-tuple-element.364, bf16[512,3,12,64]{0,3,2,1:T(8,128)(2,1)S(1)} %dynamic-slice_bitcast_fusion.7), kind=kOutput, calls=%fused_computation.14.clone.1 | convolution fusion | flops 418375680 | bytes 39378944 | tf_op jit(solution)/shard_map/while/body/eval_jaxpr/qhd,khd->hqk/dot_general | solution.py:166
  643.7 19.0 %fusion.106 = (bf16[12,512,512]{1,2,0:T(8,128)(2,1)S(1)}, f32[12,512,512]{1,2,0:T(8,128)}) fusion(f32[12,512,512]{1,2,0:T(8,128)} %get-tuple-element.320, f32[12,512,512]{1,2,0:T(8,128)} %fusion.105, f32[12,512]{1,0:T(8,128)} %get-tuple-element.321, f32[12,512,512]{1,2,0:T(8,128)} %get-tuple-element.352, pred[]{:T(512)S(6)} %compare.3), kind=kLoop, calls=%fused_computation.18.clone.1 | loop fusion | flops 15728640 | bytes 56647680 | tf_op jit(solution)/shard_map/while/body/eval_jaxpr/convert_element_type | solution.py:181
  693.6 12.8 %copy.69 = f32[12,512,512]{2,1,0:T(8,128)} copy(f32[12,512,512]{1,2,0:T(8,128)} %get-tuple-element.85) | data formatting | bytes 25165824 | tf_op jit(solution)/shard_map/while | solution.py:191
  706.4 11.2 broadcast_multiply_fusion
  717.6 10.7 fusion.59
  728.3 10.2 fusion.58
  739.1 22.0 %psum.99 = f32[768]{0:T(1024)} all-reduce(f32[768]{0:T(1024)S(1)} %copy-done.28), channel_id=1, replica_groups=mesh['dp'=8,'mp'=4] {'dp'}, use_global_device_ids=true, to_apply=%region_31.32 | all-reduce | flops 768 | bytes 6144 | tf_op jit(solution)/shard_map/psum | solution.py:146
  784.2 38.8 %all-reduce = (f32[768]{0:T(1024)}, f32[768]{0:T(1024)}, f32[768]{0:T(1024)}, f32[768]{0:T(1024)}, f32[768]{0:T(1024)}, /*index=5*/f32[768]{0:T(1024)}, f32[768]{0:T(1024)}, f32[768]{0:T(1024)}) all-reduce(f32[768]{0:T(1024)S(1)} %get-tuple-element.167, f32[768]{0:T(1024)S(1)} %get-tuple-element.166, ...), channel_id=1, replica_groups=mesh['dp'=8,'mp'=4] {'dp','mp'}, use_global_device_ids=true, to_apply=%region_19.20 | all-reduce | flops 6144 | bytes 49152 | tf_op jit(solution)/shard_map/psum | solution.py:222
  822.9 62.8 %all-reduce.6.cloned.1.call-done = (f32[768,2304]{0,1:T(8,128)}, f32[768,768]{1,0:T(8,128)}) async-done(((f32[768,2304]{0,1:T(8,128)}, f32[768,768]{1,0:T(8,128)}), (f32[768,2304]{0,1:T(8,128)}, f32[768,768]{1,0:T(8,128)})) %all-reduce.6.cloned.1.call-update) | async-done | bytes 9437200 | tf_op jit(solution)/shard_map/psum | solution.py:222
  893.7 155.0 %reduce-scatter.8.cloned.1.call-done = f32[12,16,512]{2,1,0:T(8,128)} async-done(((f32[12,512,512]{2,1,0:T(8,128)}), f32[12,16,512]{2,1,0:T(8,128)}) %reduce-scatter.8.cloned.1.call-update) | async-done | bytes 393232 | tf_op jit(solution)/shard_map/reduce_scatter | solution.py:197
  1050.6 172.0 %all-reduce.8.cloned.1.call-done = (f32[768,768]{1,0:T(8,128)}, f32[768,768]{1,0:T(8,128)}) async-done(((f32[768,768]{1,0:T(8,128)}, f32[768,768]{1,0:T(8,128)}), (f32[768,768]{1,0:T(8,128)}, f32[768,768]{1,0:T(8,128)})) %all-reduce.8.cloned.1.call-update) | async-done | bytes 4718608 | tf_op jit(solution)/shard_map/psum | solution.py:146
  (194 shorter events, 240.3 us)
Async XLA Ops:
  7.2 6.3 copy-start
  7.2 103.1 %all-gather.4.cloned.1.call-start = ((), (), s32[]{:S(2)}) async-start(), calls=%async_computation.3 | async-start | bytes 12976128 | tf_op jit(solution)/shard_map/all_gather | solution.py:69
  9.5 214.6 %all-gather.6.cloned.1.call-start = ((), (), s32[]{:S(2)}) async-start(), calls=%async_computation.4 | async-start | bytes 7864320 | tf_op jit(solution)/shard_map/all_gather | solution.py:108
  36.3 6.2 copy-start.30
  36.3 6.8 copy-start.31
  133.5 38.1 %copy-start.27 = (f32[768]{0:T(1024)S(1)}, f32[768]{0:T(1024)}, u32[]{:S(2)}) copy-start(f32[768]{0:T(1024)} %convert_element_type.107) | copy-start | bytes 9220
  135.4 6.5 copy-start.4
  154.4 6.5 copy-start.4
  178.9 190.4 %reduce-scatter.4.cloned.1.call-start = ((), (), s32[]{:S(2)}) async-start(), calls=%async_computation.5 | async-start | bytes 15728640 | tf_op jit(solution)/shard_map/reduce_scatter | solution.py:113
  224.1 38.1 %copy-start.33 = (bf16[768,768]{1,0:T(8,128)(2,1)S(1)}, bf16[768,768]{1,0:T(8,128)(2,1)}, u32[]{:S(2)}) copy-start(bf16[768,768]{1,0:T(8,128)(2,1)} %param.31) | copy-start | bytes 3538948
  270.2 153.4 %all-gather.8.cloned.1.call-start = ((), (), s32[]{:S(2)}) async-start(), calls=%async_computation.6 | async-start | bytes 7864320 | tf_op jit(solution)/shard_map/all_gather | solution.py:128
  377.1 169.5 %reduce-scatter.6.cloned.1.call-start = ((), (), s32[]{:S(2)}) async-start(), calls=%async_computation.7 | async-start | bytes 15728640 | tf_op jit(solution)/shard_map/reduce_scatter | solution.py:140
  423.6 15.7 %copy-start.34 = (bf16[768,768]{1,0:T(8,128)(2,1)S(1)}, bf16[768,768]{1,0:T(8,128)(2,1)}, u32[]{:S(2)}) copy-start(bf16[768,768]{1,0:T(8,128)(2,1)} %param.29) | copy-start | bytes 3538948
  447.3 438.4 %all-reduce.6.cloned.1.call-start = ((), (), s32[]{:S(2)}) async-start(), calls=%async_computation.9 | async-start | bytes 18874368 | tf_op jit(solution)/shard_map/psum | solution.py:222
  546.6 8.4 copy-start.6
  573.6 6.6 copy-start.2
  573.8 6.4 copy-start.18
  595.0 16.0 %copy-start.3 = (bf16[512,3,12,64]{0,3,2,1:T(8,128)(2,1)S(1)}, bf16[512,3,12,64]{0,3,2,1:T(8,128)(2,1)}, u32[]{:S(2)}) copy-start(bf16[512,3,12,64]{0,3,2,1:T(8,128)(2,1)} %copy-done.2) | copy-start | bytes 7077892 | tf_op jit(solution)/shard_map/while
  622.3 6.6 copy-start.2
  622.5 6.4 copy-start.18
  643.7 19.0 %copy-start.3 = (bf16[512,3,12,64]{0,3,2,1:T(8,128)(2,1)S(1)}, bf16[512,3,12,64]{0,3,2,1:T(8,128)(2,1)}, u32[]{:S(2)}) copy-start(bf16[512,3,12,64]{0,3,2,1:T(8,128)(2,1)} %copy-done.2) | copy-start | bytes 7077892 | tf_op jit(solution)/shard_map/while
  693.6 355.1 %reduce-scatter.8.cloned.1.call-start = ((), (), s32[]{:S(2)}) async-start(), calls=%async_computation.8 | async-start | bytes 12976128 | tf_op jit(solution)/shard_map/reduce_scatter | solution.py:197
  717.6 505.0 %all-reduce.8.cloned.1.call-start = ((), (), s32[]{:S(2)}) async-start(), calls=%async_computation.10 | async-start | bytes 9437184 | tf_op jit(solution)/shard_map/psum | solution.py:146
  761.2 7.3 copy-start.12
  (30 other events, 97.6 us)
Sparse Core Ops, SparseCore 0:
  11.5 98.7 all-gather.3
  179.1 44.9 all-gather.5
  270.3 99.0 reduce-scatter.3
  377.2 46.3 all-gather.7
  447.5 99.0 reduce-scatter.5
  693.7 192.0 all-reduce.5
  892.8 155.8 reduce-scatter.7
  1053.5 169.0 all-reduce.7
where the time goes:
time: 1250 us; the launch traced here: 1240 us
  waiting for transfers between devices  738 us (59%)
  matrix products  192 us (15%)
  local copies, waits for them, and re-layouts  123 us (10%)
  other arithmetic  106 us (8%)
  blocking collectives  60.8 us (5%)
  between operations  14.9 us (1%)
    psum x1, waiting for transfers between devices, body(): lax.psum((part_in, part_bias, part_down), 'dp')  172 us
    reduce_scatter x1, waiting for transfers between devices, body(): lax.psum_scatter(MASK_SCALE * mask_term, ('dp', 'mp'), scatter_dimension=...  155 us
    reduce_scatter x1, waiting for transfers between devices, body(): lax.psum_scatter(jnp.dot(grad_pre, w_in, preferred_element_type=jnp.float...  97.9 us
    reduce_scatter x1, waiting for transfers between devices, body(): lax.psum_scatter(jnp.dot(active, w_down, preferred_element_type=jnp.float...  93.8 us
    all_gather x1, waiting for transfers between devices, body(): mask_all = lax.all_gather(mask_own, ('dp', 'mp'), axis=1, tiled=True)  66.6 us
    psum x1, waiting for transfers between devices, body(): lax.psum((grad_w_qkv, grad_w_out, grad_bias_q, grad_bias_v, grad_bias_out...  62.8 us
    all_gather x1, waiting for transfers between devices, body(): grad_rows = lax.all_gather(grad_branch, 'mp', axis=0, tiled=True)  46.5 us
    all_gather x1, waiting for transfers between devices, body(): ffn_inputs = lax.all_gather(first_low, 'mp', axis=0, tiled=True)  43.8 us
  transfers between devices with their start and end apart: 8, of which 8 were waited for; matrix products, arithmetic and copies ran while one was open for 10% of the time, Pallas kernels for 0%

commit v1 on v0

v1 whole, which is shorter than its diff:
```python
import functools

import jax
import jax.numpy as jnp
from jax import lax
from jax.experimental import pallas as pl
from jax.experimental.pallas import tpu as pltpu
from jax.sharding import PartitionSpec as P

MASK_SCALE = 4.0

BF = jnp.bfloat16
F32 = jnp.float32
NT = (((1,), (1,)), ((), ()))
NN = (((1,), (0,)), ((), ()))
TN = (((0,), (0,)), ((), ()))
VMEM_LIMIT = 56 * 1024 * 1024
SIZES = (8, 4, 4)

def cost(us):
    return pl.CostEstimate(flops=int(us * 1.0e9), transcendentals=0, bytes_accessed=int(us * 2.0e6))

def dot(a, b, dims=NN):
    return lax.dot_general(a, b, dims, preferred_element_type=F32)

def identity(n):
    return (lax.broadcasted_iota(jnp.int32, (n, n), 0) == lax.broadcasted_iota(jnp.int32, (n, n), 1)).astype(F32).astype(BF)

def params(*sem):
    return pltpu.CompilerParams(dimension_semantics=sem or None, vmem_limit_bytes=VMEM_LIMIT)

def place_mask(order_ref, pieces, codes, bias, eye):
    slots = 16
    rows = codes.shape[0] // slots
    for head in range(2):
        for slot in range(slots):
            group = pieces[head * 4 + slot // 4]
            start = pl.multiple_of(order_ref[head * slots + slot] * rows, rows)
            codes[pl.ds(start, rows), :] = group[slot % 4]
        turned = dot(eye, codes[...], NT)
        bias[head] = jnp.where(turned > 0.0, turned - 4.0, turned)

def halves(seqs, length, lane):
    half = seqs // 2
    return [pl.BlockSpec((length, lane), lambda s, *_: (jnp.minimum(s, half - 1), 0)),
            pl.BlockSpec((length, lane), lambda s, *_: (jnp.maximum(s - half, 0), 0))]

def attend_body(order_ref, q_ref, k_ref, v_ref, *refs):
    pieces, (own_ref, other_ref, total_ref), (codes, bias) = refs[:8], refs[8:11], refs[11:]
    length = codes.shape[0]
    @pl.when(pl.program_id(0) == 0)
    def _():
        place_mask(order_ref, pieces, codes, bias, identity(length))
    half = q_ref.shape[2] // 2
    lanes = lax.broadcasted_iota(jnp.int32, (1, 2 * half), 1)
    query, keys = q_ref[0], k_ref[0]
    values_t = v_ref[0].T
    outs = []
    for head in range(2):
        own = (lanes >= half) if head else (lanes < half)
        scores = dot(keys, jnp.where(own, query, jnp.zeros_like(query)), NT) + bias[head]
        highest = jnp.max(scores, axis=0, keepdims=True)
        powers = jnp.exp(scores - highest)
        summed = jnp.sum(powers, axis=0, keepdims=True)
        probs = (powers * (1.0 / summed)).astype(BF)
        outs.append(dot(values_t[head * half:(head + 1) * half], probs))
        total_ref[0, head:head + 1, :] = highest + jnp.log(summed)
    mixed = jnp.concatenate(outs, axis=0).T.astype(BF)
    step = pl.program_id(0)
    @pl.when(step < pl.num_programs(0) // 2)
    def _():
        own_ref[...] = mixed
    @pl.when(step >= pl.num_programs(0) // 2)
    def _():
        other_ref[...] = mixed

def attend(pair, order, qkv, pieces):
    _, tokens, width = qkv.shape
    length = pieces[0].shape[2]
    seqs = tokens // length
    lane = 128
    def part(which):
        return pl.BlockSpec((1, length, lane), lambda s, o: (which, s, pair))
    whole = [pl.BlockSpec(p.shape, lambda s, o: (0, 0, 0)) for p in pieces]
    return pl.pallas_call(
        attend_body,
        grid_spec=pltpu.PrefetchScalarGridSpec(
            num_scalar_prefetch=1, grid=(seqs,),
            in_specs=[part(0), part(1), part(2), *whole],
            out_specs=[*halves(seqs, length, lane), pl.BlockSpec((1, 8, length), lambda s, o: (s, 0, 0))],
            scratch_shapes=[pltpu.VMEM((length, length), BF), pltpu.VMEM((2, length, length), F32)],
        ),
        out_shape=[jax.ShapeDtypeStruct((tokens // 2, lane), BF)] * 2 + [jax.ShapeDtypeStruct((seqs, 8, length), F32)],
        compiler_params=params("arbitrary"),
        cost_estimate=cost(9),
        name="attend",
    )(order, qkv, qkv, qkv, *pieces)

def attend_back_body(order_ref, q_ref, k_ref, v_ref, mixed_own, mixed_other, ga_own, ga_other, wout_ref, total_ref, *refs):
    pieces, (own_ref, other_ref), mask_outs, (codes, bias, acc) = refs[:8], refs[8:10], refs[10:16], refs[16:]
    length = codes.shape[0]
    step = pl.program_id(0)
    @pl.when(step == 0)
    def _():
        place_mask(order_ref, pieces, codes, bias, identity(length))
        acc[...] = jnp.zeros_like(acc)
    half = q_ref.shape[2] // 2
    lanes = lax.broadcasted_iota(jnp.int32, (1, 2 * half), 1)
    query, keys, values = q_ref[0], k_ref[0], v_ref[0]
    keys_t = keys.T
    is_own = step < pl.num_programs(0) // 2
    grad = dot(jnp.where(is_own, ga_own[...], ga_other[...]), wout_ref[...], NT).astype(BF)
    mixed = jnp.where(is_own, mixed_own[...], mixed_other[...])
    inner = (grad.astype(F32) * mixed.astype(F32)).T
    dq, dk, dv = [], [], []
    for head in range(2):
        own = (lanes >= half) if head else (lanes < half)
        scores = dot(keys, jnp.where(own, query, jnp.zeros_like(query)), NT) + bias[head]
        probs = jnp.exp(scores - total_ref[0, head:head + 1, :])
        delta = jnp.sum(inner[head * half:(head + 1) * half], axis=0, keepdims=True)
        grad_probs = dot(values, jnp.where(own, grad, jnp.zeros_like(grad)), NT)
        grad_scores = probs * (grad_probs - delta)
        acc[head] += grad_scores
        low = grad_scores.astype(BF)
        dv.append(dot(probs.astype(BF), grad))
        dk.append(dot(low, query))
        dq.append(dot(keys_t[head * half:(head + 1) * half], low))
    first = lanes < half
    result = jnp.concatenate([(jnp.concatenate(dq, axis=0).T * 0.125).astype(BF),
                              jnp.where(first, dk[0], dk[1]).astype(BF),
                              jnp.where(first, dv[0], dv[1]).astype(BF)], axis=1)
    @pl.when(is_own)
    def _():
        own_ref[...] = result
    @pl.when(jnp.logical_not(is_own))
    def _():
        other_ref[...] = result
    @pl.when(step == pl.num_programs(0) - 1)
    def _():
        eye = identity(length)
        rows = length // 16
        for head in range(2):
            turned = dot(eye, acc[head].astype(BF), NT)
            acc[head] = turned
            at = 16
            for i, size in enumerate(SIZES):
                at -= size
                for j in range(size):
                    start = pl.multiple_of(order_ref[head * 16 + at + j] * rows, rows)
                    mask_outs[head * 3 + i][j] = acc[head, pl.ds(start, rows), :].astype(BF)

def attend_back(pair, order, qkv, mixed, grad_attn, w_out_own, total, pieces):
    _, tokens, width = qkv.shape
    length = pieces[0].shape[2]
    seqs = tokens // length
    rows = length // 16
    lane = 128
    wide = grad_attn[0].shape[1]
    def part(which):
        return pl.BlockSpec((1, length, lane), lambda s, o: (which, s, pair))
    whole = [pl.BlockSpec(p.shape, lambda s, o: (0, 0, 0)) for p in pieces]
    sizes = SIZES * 2
    return pl.pallas_call(
        attend_back_body,
        grid_spec=pltpu.PrefetchScalarGridSpec(
            num_scalar_prefetch=1, grid=(seqs,),
            in_specs=[part(0), part(1), part(2), *halves(seqs, length, lane), *halves(seqs, length, wide),
                      pl.BlockSpec((lane, wide), lambda s, o: (pair, 0)),
                      pl.BlockSpec((1, 8, length), lambda s, o: (s, 0, 0)), *whole],
            out_specs=halves(seqs, length, 3 * lane) + [pl.BlockSpec((n, rows, length), lambda s, o: (0, 0, 0)) for n in sizes],
            scratch_shapes=[pltpu.VMEM((length, length), BF), pltpu.VMEM((2, length, length), F32), pltpu.VMEM((2, length, length), F32)],
        ),
        out_shape=[jax.ShapeDtypeStruct((tokens // 2, 3 * lane), BF)] * 2 + [jax.ShapeDtypeStruct((n, rows, length), BF) for n in sizes],
        compiler_params=params("arbitrary"),
        cost_estimate=cost(13),
        name="attend_back",
    )(order, qkv, qkv, qkv, *mixed, *grad_attn, w_out_own, total, *pieces)

def full(shape):
    return pl.BlockSpec(shape, lambda *_: (0,) * len(shape))

def project_body(core_ref, own_ref, other_ref, w_ref, shift_ref, out_ref):
    third = pl.program_id(0)
    scale = jnp.where(third == 0, 0.125, 1.0)
    rows = own_ref.shape[0]
    for i, ref in enumerate((own_ref, other_ref)):
        value = (dot(ref[...], w_ref[...]) + shift_ref[...]).astype(BF)
        out_ref[0, i * rows:(i + 1) * rows] = (value.astype(F32) * scale).astype(BF)

def project(core, own_tokens, other_tokens, w_qkv, shift):
    rows, width = own_tokens.shape
    own = width // 2
    return pl.pallas_call(
        project_body,
        grid_spec=pltpu.PrefetchScalarGridSpec(
            num_scalar_prefetch=1, grid=(3,),
            in_specs=[full((rows, width)), full((rows, width)),
                      pl.BlockSpec((width, own), lambda t, c: (0, 2 * t + c[0])),
                      pl.BlockSpec((1, own), lambda t, c: (0, 2 * t + c[0]))],
            out_specs=pl.BlockSpec((1, 2 * rows, own), lambda t, c: (t, 0, 0)),
        ),
        out_shape=jax.ShapeDtypeStruct((3, 2 * rows, own), BF),
        compiler_params=params("arbitrary"),
        cost_estimate=cost(8),
        name="project",
    )(core, own_tokens, other_tokens, w_qkv, shift)

def erf_parts(u):
    x = jnp.abs(u) * 0.7071067811865476
    t = 1.0 / (1.0 + 0.3275911 * x)
    e = jnp.exp(-0.5 * u * u)
    poly = t * (0.127414796 + t * (-0.142248368 + t * (0.7107068705 + t * (-0.7265760135 + t * 0.5307027145))))
    tail = poly * e
    return jnp.where(u < 0.0, tail, 1.0 - tail), e * 0.3989422804014327

def row_mean(v):
    return jnp.mean(v, axis=-1, keepdims=True)

def ffn_body(*refs):
    tok_ref, gout_ref = refs[:2]
    mixed, (wout_ref, vec_ref, bin_ref), w_in, w_down = refs[2:8], refs[8:11], refs[11:15], refs[15:19]
    out_ref, low_ref, active_ref, slope_ref, gsec_ref, gbr_ref, norm_ref, inv_ref, sums_ref = refs[19:]
    bias_out, gain1, shift1, bias_down, gain2, shift2 = (vec_ref[i:i + 1] for i in range(6))
    gathered = jnp.concatenate([m[...] for m in mixed], axis=1)
    value = tok_ref[...].astype(F32) + dot(gathered, wout_ref[...]) + bias_out
    centered = value - row_mean(value)
    inverse = lax.rsqrt(row_mean(centered * centered) + 1e-12)
    normal = centered * inverse
    norm_ref[...] = normal
    inv_ref[...] = jnp.broadcast_to(inverse, inv_ref.shape)
    first = normal * gain1 + shift1
    low = first.astype(BF)
    low_ref[...] = low
    width = low.shape[1]
    branch = first + bias_down
    for b in range(4):
        pre = dot(low, w_in[b][...], NT) + bin_ref[b:b + 1]
        cum, dens = erf_parts(pre)
        act = (pre * cum).astype(BF)
        active_ref[:, b * width:(b + 1) * width] = act
        slope_ref[:, b * width:(b + 1) * width] = (cum + pre * dens).astype(slope_ref.dtype)
        branch += dot(act, w_down[b][...])
    centered = branch - row_mean(branch)
    inverse = lax.rsqrt(row_mean(centered * centered) + 1e-12)
    normal = centered * inverse
    out_ref[...] = (normal * gain2 + shift2).astype(BF)
    grad = gout_ref[...].astype(F32)
    inner = grad * gain2
    back = inverse * (inner - row_mean(inner) - normal * row_mean(inner * normal))
    gsec_ref[...] = back
    gbr_ref[...] = back.astype(BF)
    @pl.when(pl.program_id(0) == 0)
    def _():
        sums_ref[...] = jnp.zeros_like(sums_ref)
    total = lambda v: jnp.sum(v, axis=0, keepdims=True)
    sums_ref[0:1] += total(grad * normal)
    sums_ref[1:2] += total(grad)
    sums_ref[2:3] += total(back)

def ffn(tokens, grad_out, mixed, w_out, vecs, b_in, w_in, w_down, tile=256):
    rows, width = tokens.shape
    hidden = 4 * width
    row = lambda n: pl.BlockSpec((tile, n), lambda i: (i, 0))
    sds = jax.ShapeDtypeStruct
    return pl.pallas_call(
        ffn_body,
        grid=(rows // tile,),
        in_specs=[row(width), row(width)] + [row(m.shape[1]) for m in mixed]
        + [full(a.shape) for a in (w_out, vecs, b_in, *w_in, *w_down)],
        out_specs=[row(width), row(width), row(hidden), row(hidden), row(width), row(width), row(width), row(128), full((8, width))],
        out_shape=[sds((rows, width), BF), sds((rows, width), BF), sds((rows, hidden), BF), sds((rows, hidden), BF),
                   sds((rows, width), F32), sds((rows, width), BF), sds((rows, width), F32), sds((rows, 128), F32), sds((8, width), F32)],
        compiler_params=params("arbitrary"),
        cost_estimate=cost(30),
        name="ffn",
    )(tokens, grad_out, *mixed, w_out, vecs, b_in, *w_in, *w_down)

def ffn_back_body(*refs):
    gbr_ref, slope_ref, gsec_ref, norm_ref, inv_ref, vec_ref = refs[:6]
    w_in, w_down = refs[6:10], refs[10:14]
    gpre_ref, gone_ref, gattn_ref, sums_ref = refs[14:]
    gain1 = vec_ref[1:2]
    @pl.when(pl.program_id(0) == 0)
    def _():
        sums_ref[...] = jnp.zeros_like(sums_ref)
    total = lambda v: jnp.sum(v, axis=0, keepdims=True)
    width = gbr_ref.shape[1]
    grad = gsec_ref[...]
    low = gbr_ref[...]
    for b in range(4):
        at = slice(b * width, (b + 1) * width)
        gpre = (dot(low, w_down[b][...], NT) * slope_ref[:, at].astype(F32)).astype(BF)
        gpre_ref[:, at] = gpre
        sums_ref[4 + b:5 + b] += total(gpre.astype(F32))
        grad += dot(gpre, w_in[b][...])
    normal, inverse = norm_ref[...], inv_ref[:, 0:1]
    inner = grad * gain1
    back = inverse * (inner - row_mean(inner) - normal * row_mean(inner * normal))
    gone_ref[...] = back
    gattn_ref[...] = back.astype(BF)
    sums_ref[0:1] += total(grad * normal)
    sums_ref[1:2] += total(grad)
    sums_ref[2:3] += total(back)

def ffn_back(grad_branch, slope, grad_second, normal, inverse, vecs, w_in, w_down, tile=256):
    rows, width = grad_branch.shape
    hidden = 4 * width
    row = lambda n: pl.BlockSpec((tile, n), lambda i: (i, 0))
    sds = jax.ShapeDtypeStruct
    return pl.pallas_call(
        ffn_back_body,
        grid=(rows // tile,),
        in_specs=[row(width), row(hidden), row(width), row(width), row(128)] + [full(a.shape) for a in (vecs, *w_in, *w_down)],
        out_specs=[row(hidden), row(width), row(width), full((8, width))],
        out_shape=[sds((rows, hidden), BF), sds((rows, width), F32), sds((rows, width), BF), sds((8, width), F32)],
        compiler_params=params("arbitrary"),
        cost_estimate=cost(18),
        name="ffn_back",
    )(grad_branch, slope, grad_second, normal, inverse, vecs, *w_in, *w_down)

def outer_send_body(a_ref, b_ref, out_ref):
    out_ref[0] = dot(a_ref[...], b_ref[...], TN).astype(BF)

def outer_send(a, b):
    rows, width = b.shape
    return pl.pallas_call(
        outer_send_body,
        grid=(2,),
        in_specs=[pl.BlockSpec((rows, width), lambda i: (0, 2 * i + 1)), full((rows, width))],
        out_specs=pl.BlockSpec((1, width, width), lambda i: (i, 0, 0)),
        out_shape=jax.ShapeDtypeStruct((2, width, width), BF),
        compiler_params=params("arbitrary"),
        cost_estimate=cost(6),
        name="outer_send",
    )(a, b)

def outer_keep_body(a_ref, b_ref, add_ref, keep_ref, send_ref):
    value = dot(a_ref[...], b_ref[...], TN) + add_ref[0].astype(F32)
    @pl.when(pl.program_id(0) == 0)
    def _():
        send_ref[...] = value.astype(BF)
    @pl.when(pl.program_id(0) == 1)
    def _():
        keep_ref[...] = value

def outer_keep(a, b, add):
    rows, width = b.shape
    return pl.pallas_call(
        outer_keep_body,
        grid=(2,),
        in_specs=[pl.BlockSpec((rows, width), lambda i: (0, 2 - 2 * i)), full((rows, width)),
                  pl.BlockSpec((1, width, width), lambda i: (1 - i, 0, 0))],
        out_specs=[full((width, width)), full((width, width))],
        out_shape=[jax.ShapeDtypeStruct((width, width), F32), jax.ShapeDtypeStruct((width, width), BF)],
        compiler_params=params("arbitrary"),
        cost_estimate=cost(7),
        name="outer_keep",
    )(a, b, add)

def outer_slots_body(order_ref, a_own, a_other, *refs):
    bs, outs, (sums_ref, acc) = refs[:-5], refs[-5:-2], refs[-2:]
    count = len(bs) // 2
    own, other = (jnp.concatenate([r[...] for r in part], axis=1) if count > 1 else part[0][...] for part in (bs[:count], bs[count:]))
    acc[...] = dot(a_own[...], own, TN) + dot(a_other[...], other, TN)
    sums_ref[0:1] = jnp.sum(own.astype(F32), axis=0, keepdims=True) + jnp.sum(other.astype(F32), axis=0, keepdims=True)
    at = 16
    rows = acc.shape[0] // 16
    for out, size in zip(outs, SIZES):
        at -= size
        for j in range(size):
            start = pl.multiple_of(order_ref[at + j] * rows, rows)
            out[j] = acc[pl.ds(start, rows), :].astype(BF)

def outer_slots(order, a, own, other):
    width = a[0].shape[1]
    wide = sum(b.shape[1] for b in own)
    shapes = [(n, width // 16, wide) for n in SIZES]
    return pl.pallas_call(
        outer_slots_body,
        grid_spec=pltpu.PrefetchScalarGridSpec(
            num_scalar_prefetch=1, grid=(1,),
            in_specs=[full(x.shape) for x in (*a, *own, *other)],
            out_specs=[full(s) for s in shapes] + [full((8, wide))],
            scratch_shapes=[pltpu.VMEM((width, wide), F32)],
        ),
        out_shape=[jax.ShapeDtypeStruct(s, BF) for s in shapes] + [jax.ShapeDtypeStruct((8, wide), F32)],
        compiler_params=params("arbitrary"),
        cost_estimate=cost(5.6),
        name="outer_slots",
    )(order, *a, *own, *other)

def grad_tokens_body(*refs):
    pieces, one_ref, w_ref, out_ref = refs[:6], refs[6], refs[7], refs[8]
    wide = jnp.concatenate([r[...] for r in pieces], axis=1)
    out_ref[...] = (one_ref[...] + dot(wide, w_ref[...], NT)).astype(BF)

def grad_tokens(pieces, grad_one, w, tile=256):
    rows, width = grad_one.shape
    row = lambda n: pl.BlockSpec((tile, n), lambda i: (i, 0))
    return pl.pallas_call(
        grad_tokens_body,
        grid=(rows // tile,),
        in_specs=[row(p.shape[1]) for p in pieces] + [row(width), full(w.shape)],
        out_specs=row(width),
        out_shape=jax.ShapeDtypeStruct((rows, width), BF),
        compiler_params=params("arbitrary"),
        cost_estimate=cost(6),
        name="grad_tokens",
    )(*pieces, grad_one, w)

def place_rows_body(order_ref, *refs):
    pieces, out_ref = refs[:-1], refs[-1]
    rows = pieces[0].shape[1]
    at = 0
    for piece in pieces:
        for j in range(piece.shape[0]):
            start = pl.multiple_of(order_ref[at] * rows, rows)
            out_ref[pl.ds(start, rows), :] = piece[j].astype(F32)
            at += 1

def place_rows(order, pieces):
    count = sum(p.shape[0] for p in pieces)
    _, rows, width = pieces[0].shape
    return pl.pallas_call(
        place_rows_body,
        grid_spec=pltpu.PrefetchScalarGridSpec(
            num_scalar_prefetch=1, grid=(1,), in_specs=[full(p.shape) for p in pieces], out_specs=full((count * rows, width))),
        out_shape=jax.ShapeDtypeStruct((count * rows, width), F32),
        compiler_params=params("arbitrary"),
        cost_estimate=cost(2),
        name="place_rows",
    )(order, *pieces)

def place_heads_body(order_ref, core_ref, *refs):
    pieces, out_ref = refs[:-1], refs[-1]
    width = out_ref.shape[0]
    per = len(pieces) // 6
    for pair in range(3):
        for side in range(2):
            own = pieces[(pair * 2 + side) * per:(pair * 2 + side + 1) * per]
            rows = own[0].shape[1]
            at = 0
            head = core_ref[side] * 3 + pair
            for piece in own:
                for j in range(piece.shape[0]):
                    start = pl.multiple_of(order_ref[pair * 16 + at] * rows, rows)
                    value = piece[j].astype(F32)
                    for third in range(3):
                        column = pl.multiple_of(third * width + head * 128, 128)
                        out_ref[pl.ds(start, rows), pl.ds(column, 128)] = value[:, third * 128:(third + 1) * 128]
                    at += 1

def place_heads(order, core, pieces):
    width = 16 * pieces[0].shape[1]
    return pl.pallas_call(
        place_heads_body,
        grid_spec=pltpu.PrefetchScalarGridSpec(
            num_scalar_prefetch=2, grid=(1,), in_specs=[full(p.shape) for p in pieces], out_specs=full((width, 3 * width))),
        out_shape=jax.ShapeDtypeStruct((width, 3 * width), F32),
        compiler_params=params("arbitrary"),
        cost_estimate=cost(5),
        name="place_heads",
    )(order, core, *pieces)

def place_turned_body(order_ref, core_ref, *refs):
    pieces, out_ref, acc = refs[:-2], refs[-2], refs[-1]
    per = len(pieces) // 2
    wide = acc.shape[1]
    for side in range(2):
        at = 0
        for piece in pieces[side * per:(side + 1) * per]:
            rows = piece.shape[1]
            for j in range(piece.shape[0]):
                start = pl.multiple_of(order_ref[at] * rows, rows)
                acc[pl.ds(start, rows), :] = piece[j].astype(F32)
                at += 1
        start = pl.multiple_of(core_ref[side] * wide, wide)
        out_ref[pl.ds(start, wide), :] = acc[...].T

def place_turned(order, core, pieces):
    _, rows, wide = pieces[0].shape
    width = 16 * rows
    return pl.pallas_call(
        place_turned_body,
        grid_spec=pltpu.PrefetchScalarGridSpec(
            num_scalar_prefetch=2, grid=(1,), in_specs=[full(p.shape) for p in pieces], out_specs=full((2 * wide, width)),
            scratch_shapes=[pltpu.VMEM((width, wide), F32)]),
        out_shape=jax.ShapeDtypeStruct((2 * wide, width), F32),
        compiler_params=params("arbitrary"),
        cost_estimate=cost(4),
        name="place_turned",
    )(order, core, *pieces)


AXES = ("dp", "mp")
CORE, ROW, COLUMN, DEPTH = 1, 2, 4, 8


class Links:
    def __init__(self, dp, mp):
        self.dp, self.mp = dp, mp
        self.direct = dp == 8 and mp == 4
        self.at_dp, self.at_mp = lax.axis_index("dp"), lax.axis_index("mp")
        self.core, self.row = self.at_mp % 2, self.at_mp // 2
        slot = jnp.arange(16)
        z, low, high = slot & 3, (slot >> 2) & 1, slot >> 3
        if self.direct:
            def chip(x, y):
                return ((self.at_dp ^ (x | (z << 1))) * 2 + (self.row ^ y)).astype(jnp.int32)
            self.order_a, self.order_b = chip(low, high), chip(high, low)
            self.eighths = (self.at_dp ^ (((slot[:8] >> 2) & 1) | ((slot[:8] & 3) << 1))).astype(jnp.int32)
        else:
            self.order_a = self.order_b = slot.astype(jnp.int32)
            self.eighths = slot[:8].astype(jnp.int32)
        self.cores = jnp.stack([self.core, 1 - self.core]).astype(jnp.int32)

    def swap(self, value, bits):
        count = self.dp * self.mp
        return lax.ppermute(value, AXES, [(i, i ^ bits) for i in range(count)])

    def add_all(self, value):
        if not self.direct:
            return lax.psum(value, AXES)
        for bits in (1, 2, 4, 8, 16):
            value = value + self.swap(value, bits)
        return value


def pick(index, first, second):
    return jnp.where(index == 0, first, second)


def mask_codes(links, code):
    heads, rows, length = code.shape
    half = heads // 2
    if not links.direct:
        whole = lax.all_gather(code, AXES, axis=1, tiled=True)
        own = lax.dynamic_slice_in_dim(whole, links.core * half, half, 0).reshape(half, 16, length // 16, length)
        return [[own[2 * p + h, 4 * i:4 * i + 4] for h in range(2) for i in range(4)] for p in range(half // 2)]
    keep = pick(links.core, code[:half], code[half:])
    came = links.swap(pick(links.core, code[half:], code[:half]), CORE)
    chip = pick(links.core, jnp.concatenate([keep, came], 1), jnp.concatenate([came, keep], 1))
    result = []
    for p in range(half // 2):
        own = chip[2 * p:2 * p + 2]
        deep = [own] + [links.swap(own, k * DEPTH) for k in (1, 2, 3)]
        pieces = []
        for h, (near, far) in enumerate(((COLUMN, ROW), (ROW, COLUMN))):
            group = jnp.stack([d[h] for d in deep])
            second = links.swap(group, near)
            pieces += [group, second, links.swap(group, far), links.swap(second, far)]
        result.append(pieces)
    return result


def scatter_slots(links, slots, far, near):
    away, mid, last = slots
    came = links.swap(away, far)
    came_mid = links.swap((mid.astype(F32) + came[4:].astype(F32)).astype(BF), near)
    total = last.astype(F32) + came[:4].astype(F32) + came_mid.astype(F32)
    own = total[0]
    for k in (1, 2, 3):
        own = own + links.swap(total[k].astype(BF), k * DEPTH).astype(F32)
    return own


def gather_slots(links, own, far, near):
    group = jnp.concatenate([own] + [links.swap(own, k * DEPTH) for k in (1, 2, 3)])
    second = links.swap(group, near)
    return [group, second, links.swap(group, far), links.swap(second, far)]


def sum_slots(links, slots, far, near):
    if not links.direct:
        whole = jnp.concatenate(slots[::-1])
        own = lax.psum(whole.astype(F32), "dp")
        parts = lax.all_gather(own, "mp")
        own = parts[links.core] + parts[links.core + 2]
        other = parts[1 - links.core] + parts[3 - links.core]
        return [own], [other]
    own = scatter_slots(links, slots, far, near)
    groups = gather_slots(links, own.astype(BF)[None], far, near)
    return groups, [links.swap(g, CORE) for g in groups]


def in_slots(links, value):
    if not links.direct:
        return value
    eighth = value.shape[0] // 8
    parts = [lax.dynamic_slice_in_dim(value, links.eighths[r] * eighth, eighth, 0) for r in range(8)]
    return jnp.concatenate(parts)


def weight_blocks(links, value, straight):
    if not links.direct:
        whole = lax.all_gather(value, "mp")
        return [whole[links.at_mp ^ k] for k in range(4)]
    own = in_slots(links, value)
    eighth = own.shape[0] // 8
    beside = links.swap(own, CORE)
    first = links.swap(own[:eighth], ROW)
    group = jnp.concatenate([first] + [links.swap(first, k * DEPTH) for k in (1, 2, 3)])
    rest = links.swap(own[4 * eighth:], ROW) if straight else links.swap(group, COLUMN)
    across = jnp.concatenate([group, rest])
    return [own, beside, across, links.swap(across, CORE)]


def hidden_gradient(links, a, b):
    sent = outer_send(a, b)
    if not links.direct:
        zero = jnp.zeros_like(sent)
        keep, near = outer_keep(a, b, zero)
        blocks = jnp.stack([keep, sent[0].astype(F32), near.astype(F32), sent[1].astype(F32)])
        blocks = jnp.stack([blocks[links.at_mp ^ k] for k in range(4)])
        mine = lax.psum_scatter(blocks, "mp", scatter_dimension=0, tiled=False)
        return lax.psum(mine, "dp")
    keep, near = outer_keep(a, b, links.swap(sent, CORE))
    eighth = keep.shape[0] // 8
    came = links.swap(near, ROW)
    total = keep + came.astype(F32)
    beside = links.swap(total[4 * eighth:].astype(BF), COLUMN)
    total = total[:4 * eighth] + beside.astype(F32)
    own = total[:eighth]
    for k in (1, 2, 3):
        own = own + links.swap(total[k * eighth:(k + 1) * eighth].astype(BF), k * DEPTH).astype(F32)
    own = own.astype(BF)[None]
    group = jnp.concatenate([own] + [links.swap(own, k * DEPTH) for k in (1, 2, 3)])
    return place_rows(links.eighths, [group, links.swap(group, COLUMN)])


def body(dp, mp, tokens, w_qkv, bias_q, bias_v, w_out, bias_out, norm1_gain, norm1_bias, w_in, bias_in, w_down, bias_down,
         norm2_gain, norm2_bias, mask_logits, mask_noise, grad_out):
    width = w_out.shape[0]
    heads, rows_own, length = mask_logits.shape
    half = heads // 2
    links = Links(dp, mp)
    core = links.core
    fraction = mask_noise.astype(F32) / 65536.0
    logit = mask_logits + jnp.log(fraction) - jnp.log(1.0 - fraction)
    mask_own = jax.nn.sigmoid(logit)
    tail = jax.nn.sigmoid(-jnp.abs(logit)) * MASK_SCALE
    pieces = mask_codes(links, jnp.where(logit < 0.0, tail, -tail).astype(BF))
    both = jnp.concatenate([links.order_a, links.order_b])
    other_tokens = links.swap(tokens, CORE)
    wide = lambda v: v.astype(F32)
    shift = jnp.concatenate([wide(bias_q), jnp.zeros((width,), F32), wide(bias_v)])[None]
    qkv = project(links.cores[:1], tokens, other_tokens, w_qkv, shift)
    own_side = lax.dynamic_slice_in_dim(w_out, core * (width // 2), width // 2, 0)
    other_side = lax.dynamic_slice_in_dim(w_out, (1 - core) * (width // 2), width // 2, 0)
    w_out_sides = jnp.concatenate([own_side, other_side])
    columns = w_qkv.reshape(width, 3, 2, 3, 128).transpose(2, 0, 3, 1, 4).reshape(2, width, 3 * width // 2)
    w_qkv_sides = jnp.concatenate([columns[core], columns[1 - core]], axis=1)
    blocks_in = weight_blocks(links, w_in, False)
    blocks_down = weight_blocks(links, w_down, True)
    if links.direct:
        own_bias = in_slots(links, bias_in)
        pair_bias = jnp.stack([own_bias, links.swap(own_bias, CORE)])
        blocks_bias = jnp.concatenate([pair_bias, links.swap(pair_bias, ROW)]).astype(F32)
    else:
        blocks_bias = lax.all_gather(bias_in, "mp")
        blocks_bias = jnp.stack([blocks_bias[links.at_mp ^ k] for k in range(4)]).astype(F32)
    mixed, totals = [], []
    for p in range(half // 2):
        own, other, total = attend(p, both, qkv, pieces[p])
        mixed.append((own, other))
        totals.append(total)
    came = [links.swap(other, CORE) for _, other in mixed]
    vecs = jnp.stack([wide(v) for v in (bias_out, norm1_gain, norm1_bias, bias_down, norm2_gain, norm2_bias)]
                     + [jnp.zeros((width,), F32)] * 2)
    out, first_low, active, slope, grad_second, grad_branch, normal, inverse, sums_a = ffn(
        tokens, grad_out, [own for own, _ in mixed] + came, w_out_sides, vecs, blocks_bias, blocks_in, blocks_down)
    grad_w_down = hidden_gradient(links, active, grad_branch)
    grad_pre, grad_one, grad_attn, sums_b = ffn_back(
        grad_branch, slope, grad_second, normal, inverse, vecs, blocks_in, blocks_down)
    other_attn = links.swap(grad_attn, CORE)
    grad_w_in = hidden_gradient(links, grad_pre, first_low)
    chip_tokens = (tokens, other_tokens)
    *slots, _ = outer_slots(links.order_b, (grad_attn, other_attn), [own for own, _ in mixed], [other for _, other in mixed])
    own, other = sum_slots(links, slots, COLUMN, ROW)
    grad_w_out = place_turned(links.order_b, links.cores, own + other)
    mask_sums, d_own, d_other, placed, column_sums, orders = [], [], [], [], [], []
    for p in range(half // 2):
        own, other, *slots = attend_back(p, both, qkv, mixed[p], (grad_attn, other_attn), own_side, totals[p], pieces[p])
        d_own.append(own)
        d_other.append(links.swap(other, CORE))
        if links.direct:
            mask_sums.append(scatter_slots(links, slots[:3], ROW, COLUMN))
            mask_sums.append(scatter_slots(links, slots[3:], COLUMN, ROW))
        else:
            mask_sums += [jnp.concatenate(slots[3 * h:3 * h + 3][::-1]).reshape(length, length) for h in range(2)]
        far, near, order = ((ROW, COLUMN, links.order_a), (COLUMN, ROW, links.order_b))[p % 2]
        *slots, sums = outer_slots(order, chip_tokens, [own], [other])
        column_sums.append(sums[0].reshape(3, 128))
        orders.append(order)
        for side in sum_slots(links, slots, far, near):
            placed += side
    grad_w_qkv = place_heads(jnp.concatenate(orders), links.cores, placed)
    grad_in = grad_tokens([*d_own, *d_other], grad_one, w_qkv_sides)
    mask_sum = jnp.stack(mask_sums)
    if links.direct:
        mine = pick(core, mask_sum[:, :rows_own], mask_sum[:, rows_own:])
        theirs = links.swap(pick(core, mask_sum[:, rows_own:], mask_sum[:, :rows_own]), CORE)
        mask_sum = pick(core, jnp.concatenate([mine, theirs]), jnp.concatenate([theirs, mine]))
    else:
        zero = jnp.zeros_like(mask_sum)
        mask_sum = pick(core, jnp.concatenate([mask_sum, zero]), jnp.concatenate([zero, mask_sum])).astype(F32)
        mask_sum = lax.psum_scatter(mask_sum, AXES, scatter_dimension=1, tiled=True)
    grad_mask_logits = mask_sum * (MASK_SCALE * mask_own * (1.0 - mask_own))
    hidden = jnp.stack([sums_b[4:8][links.at_mp ^ k] for k in range(4)])
    hidden = hidden.reshape(4, 8, width // 8)
    hidden = jnp.stack([hidden[:, (links.eighths if not links.direct else inverse_eighths(links))[r]] for r in range(8)], axis=1)
    small = jnp.concatenate([sums_a[:3], sums_b[:3], hidden.reshape(4, width)])
    small = links.add_all(small)
    grad_bias_in = small[6 + links.at_mp]
    bias = jnp.stack(column_sums, axis=1).reshape(3, width // 2)
    zero = jnp.zeros_like(bias)
    bias = links.add_all(pick(core, jnp.concatenate([bias, zero], 1), jnp.concatenate([zero, bias], 1)))
    return (out, grad_in, grad_w_qkv, bias[0], bias[2], grad_w_out, small[5], small[3], small[4], grad_w_in, grad_bias_in,
            grad_w_down, small[2], small[0], small[1], grad_mask_logits)


def inverse_eighths(links):
    place = jnp.arange(8) ^ links.at_dp
    return (((place & 1) << 2) | (place >> 1)).astype(jnp.int32)


def solution(mesh):
    both, none = ("dp", "mp"), P()
    rows, mask, split = P(both, None), P(None, both, None), P("mp", None)
    ins = (rows, none, none, none, none, none, none, none, split, P("mp"), split, none, none, none, mask, mask, rows)
    outs = (rows, rows, none, none, none, none, none, none, none, split, P("mp"), split, none, none, none, mask)
    step = functools.partial(body, mesh.shape["dp"], mesh.shape["mp"])
    return jax.shard_map(step, mesh=mesh, in_specs=ins, out_specs=outs, check_vma=False)
```

time: 1250 us -> 635 us (0.51)
  waiting for transfers between devices: 738 us -> 146 us
  Pallas kernels: 0 us -> 205 us
  matrix products: 192 us -> 0 us
  starting transfers between devices: 0.33 us -> 179 us
  other arithmetic: 106 us -> 14.3 us
  local copies, waits for them, and re-layouts: 123 us -> 60.7 us
  blocking collectives: 60.8 us -> 0 us
    reduce_scatter x3 -> x0, waiting for transfers between devices: 347 us -> none  [the longest x1 155 us: body(): lax.psum_scatter(MASK_SCALE * mask_term, ('dp', 'mp'), scatter_dimension=...]
    psum x2 -> x0, waiting for transfers between devices: 235 us -> none  [the longest x1 172 us: body(): lax.psum((part_in, part_bias, part_down), 'dp')]
    pallas_call x0 -> x22, Pallas kernels: none -> 205 us  [the longest x3 43.3 us: attend_back(): pl.pallas_call(attend_back_body, grid_spec=pltpu.PrefetchScalarGridSpec(n...]
    dot_general x26 -> x0, matrix products: 192 us -> none  [the longest x1 35.5 us: body(): lax.dot_general(ffn_inputs, full_in, CONTRACT_LAST, preferred_element_typ...]
    ppermute x0 -> x173, starting transfers between devices: none -> 179 us  [swap(): return lax.ppermute(value, AXES, [(i, i ^ bits) for i in range(count)])]
    all_gather x3 -> x0, waiting for transfers between devices: 157 us -> none  [the longest x1 66.6 us: body(): mask_all = lax.all_gather(mask_own, ('dp', 'mp'), axis=1, tiled=True)]
    ppermute x0 -> x173, waiting for transfers between devices: none -> 146 us  [swap(): return lax.ppermute(value, AXES, [(i, i ^ bits) for i in range(count)])]
    psum x2 -> x0, blocking collectives: 60.8 us -> none  [the longest x1 38.8 us: body(): lax.psum((grad_w_qkv, grad_w_out, grad_bias_q, grad_bias_v, grad_bias_out...]
  transfers between devices with their start and end apart: 8 -> 173, of which waited for: 8 -> 61; matrix products, arithmetic and copies ran while one was open for 10% -> 10% of each run, Pallas kernels for 0% -> 24%
where the time goes in v1:
time: 635 us; the launch traced here: 629 us
  Pallas kernels  205 us (32%)
  starting transfers between devices  179 us (28%)
  waiting for transfers between devices  146 us (23%)
  local copies, waits for them, and re-layouts  60.7 us (10%)
  between operations  23.7 us (4%)
  other arithmetic  14.3 us (2%)
    ppermute x173, starting transfers between devices, swap(): return lax.ppermute(value, AXES, [(i, i ^ bits) for i in range(count)])  179 us
    ppermute x173, waiting for transfers between devices, swap(): return lax.ppermute(value, AXES, [(i, i ^ bits) for i in range(count)])  146 us
    pallas_call x3, Pallas kernels, attend_back(): pl.pallas_call(attend_back_body, grid_spec=pltpu.PrefetchScalarGridSpec(n...  43.3 us
    pallas_call x1, Pallas kernels, ffn(): pl.pallas_call(ffn_body, grid=(rows // tile,), in_specs=[row(width), row(...  30.8 us
    unnamed x269, local copies, waits for them, and re-layouts  29.1 us
    pallas_call x3, Pallas kernels, attend(): pl.pallas_call(attend_body, grid_spec=pltpu.PrefetchScalarGridSpec(num_sc...  27.9 us
    pallas_call x4, Pallas kernels, outer_slots(): pl.pallas_call(outer_slots_body, grid_spec=pltpu.PrefetchScalarGridSpec(n...  22.6 us
    pallas_call x1, Pallas kernels, ffn_back(): pl.pallas_call(ffn_back_body, grid=(rows // tile,), in_specs=[row(width),...  18.7 us
  transfers between devices with their start and end apart: 173, of which 61 were waited for; matrix products, arithmetic and copies ran while one was open for 10% of the time, Pallas kernels for 24%

profile of v1, /device:TPU:0, one launch (start us, length us, event | category | flops | bytes accessed | tf_op | source)
XLA Modules:
  0.0 628.9 jit_solution(14872291440648693109)
XLA Ops:
  97.3 8.9 %project.1.q_ref.k_ref.v_ref = bf16[3,2048,384]{2,1,0:T(8,128)(2,1)} custom-call(s32[1]{0:T(128)} %bitcast.core_ref, bf16[1024,768]{1,0:T(8,128)(2,1)} %a_own.5, bf16[1024,768]{1,0:T(8,128)(2,1)} %collective-permute-done.other_ref.a_other, bf16[768,2304]{1,0:T(8,128)(2,1)} %w_ref.1, f32[1,2304]{1,0:T(1,128)} %broadcast_in_dim.26.shift_ref), custom_call_target="tpu_custom_call" | custom-call | flops 8000000000 | bytes 16000000 | tf_op jit(solution)/shard_map/project/pallas_call | solution.py:193
  111.5 9.3 %attend.5 = (bf16[1024,128]{1,0:T(8,128)(2,1)}, bf16[1024,128]{1,0:T(8,128)(2,1)}, f32[4,8,512]{2,1,0:T(8,128)}) custom-call(s32[32]{0:T(128)} %pad_add_fusion.order_ref, bf16[3,2048,384]{2,1,0:T(8,128)(2,1)} %project.1.q_ref.k_ref.v_ref, bf16[3,2048,384]{2,1,0:T(8,128)(2,1)} %project.1.q_ref.k_ref.v_ref, bf16[3,2048,384]{2,1,0:T(8,128)(2,1)} %project.1.q_ref.k_ref.v_ref, ...), custom_call_target="tpu_custom_call" | custom-call | flops 8999999488 | bytes 18000000 | tf_op jit(solution)/shard_map/attend/pallas_call | solution.py:85
  124.6 9.3 %attend.4 = (bf16[1024,128]{1,0:T(8,128)(2,1)}, bf16[1024,128]{1,0:T(8,128)(2,1)}, f32[4,8,512]{2,1,0:T(8,128)}) custom-call(s32[32]{0:T(128)} %pad_add_fusion.order_ref, bf16[3,2048,384]{2,1,0:T(8,128)(2,1)} %project.1.q_ref.k_ref.v_ref, bf16[3,2048,384]{2,1,0:T(8,128)(2,1)} %project.1.q_ref.k_ref.v_ref, bf16[3,2048,384]{2,1,0:T(8,128)(2,1)} %project.1.q_ref.k_ref.v_ref, ...), custom_call_target="tpu_custom_call" | custom-call | flops 8999999488 | bytes 18000000 | tf_op jit(solution)/shard_map/attend/pallas_call | solution.py:85
  135.7 9.3 %attend.3 = (bf16[1024,128]{1,0:T(8,128)(2,1)}, bf16[1024,128]{1,0:T(8,128)(2,1)}, f32[4,8,512]{2,1,0:T(8,128)}) custom-call(s32[32]{0:T(128)} %pad_add_fusion.order_ref, bf16[3,2048,384]{2,1,0:T(8,128)(2,1)} %project.1.q_ref.k_ref.v_ref, bf16[3,2048,384]{2,1,0:T(8,128)(2,1)} %project.1.q_ref.k_ref.v_ref, bf16[3,2048,384]{2,1,0:T(8,128)(2,1)} %project.1.q_ref.k_ref.v_ref, ...), custom_call_target="tpu_custom_call" | custom-call | flops 8999999488 | bytes 18000000 | tf_op jit(solution)/shard_map/attend/pallas_call | solution.py:85
  173.7 30.8 %ffn.1 = (bf16[1024,768]{1,0:T(8,128)(2,1)}, bf16[1024,768]{1,0:T(8,128)(2,1)}, bf16[1024,3072]{1,0:T(8,128)(2,1)}, bf16[1024,3072]{1,0:T(8,128)(2,1)}, f32[1024...) custom-call(bf16[1024,768]{1,0:T(8,128)(2,1)} %a_own.5, ...), custom_call_target="tpu_custom_call" | custom-call | flops 30000001024 | bytes 60000000 | tf_op jit(solution)/shard_map/ffn/pallas_call | solution.py:265
  204.6 18.7 %ffn_back.1 = (bf16[1024,3072]{1,0:T(8,128)(2,1)}, f32[1024,768]{1,0:T(8,128)}, bf16[1024,768]{1,0:T(8,128)(2,1)}, f32[8,768]{1,0:T(8,128)}) custom-call(bf16[1024,768]{1,0:T(8,128)(2,1)} %get-tuple-element.88.refs_0_.b_ref, bf16[1024,3072]{1,0:T(8,128)(2,1)} %get-tuple-element.89.refs_1_, f32[1024,768]{1,0:T(8,128)} %get-tuple-element.90.refs_2_, ...), custom_call_target="tpu_custom_call" | custom-call | flops 17999998976 | bytes 36000000 | tf_op jit(solution)/shard_map/ffn_back/pallas_call | solution.py:310
  249.8 14.7 %attend_back.5 = (bf16[1024,384]{1,0:T(8,128)(2,1)}, bf16[1024,384]{1,0:T(8,128)(2,1)}, bf16[8,32,512]{2,1,0:T(8,128)(2,1)}, bf16[4,32,512]{2,1,0:T(8,128)(2,1)}...) custom-call(s32[32]{0:T(128)} %pad_add_fusion.order_ref, ...), custom_call_target="tpu_custom_call" | custom-call | flops 12999999488 | bytes 26000000 | tf_op jit(solution)/shard_map/attend_back/pallas_call | solution.py:163
  264.5 5.6 outer_slots.6
  270.9 14.2 %attend_back.4 = (bf16[1024,384]{1,0:T(8,128)(2,1)}, bf16[1024,384]{1,0:T(8,128)(2,1)}, bf16[8,32,512]{2,1,0:T(8,128)(2,1)}, bf16[4,32,512]{2,1,0:T(8,128)(2,1)}...) custom-call(s32[32]{0:T(128)} %pad_add_fusion.order_ref, ...), custom_call_target="tpu_custom_call" | custom-call | flops 12999999488 | bytes 26000000 | tf_op jit(solution)/shard_map/attend_back/pallas_call | solution.py:163
  291.4 14.4 %attend_back.3 = (bf16[1024,384]{1,0:T(8,128)(2,1)}, bf16[1024,384]{1,0:T(8,128)(2,1)}, bf16[8,32,512]{2,1,0:T(8,128)(2,1)}, bf16[4,32,512]{2,1,0:T(8,128)(2,1)}...) custom-call(s32[32]{0:T(128)} %pad_add_fusion.order_ref, ...), custom_call_target="tpu_custom_call" | custom-call | flops 12999999488 | bytes 26000000 | tf_op jit(solution)/shard_map/attend_back/pallas_call | solution.py:163
  312.9 6.5 %collective-permute-start.120 = (f32[10,768]{1,0:T(8,128)S(1)}, f32[10,768]{1,0:T(8,128)S(1)}, u32[]{:S(2)}, u32[]{:S(2)}) collective-permute-start(f32[10,768]{1,0:T(8,128)S(1)} %add.418), channel_id=1, source_target_pairs={{0,8},{1,9},{2,10},{3,11},{4,12},{5,13},{6,14},{7,15},{8,0},{9,1},... | collective-permute-start | bytes 92168 | tf_op jit(solution)/shard_map/ppermute | solution.py:519
  320.9 5.8 outer_send.3
  330.2 6.0 outer_send.2
  341.4 5.8 outer_slots.7
  448.3 7.3 %outer_keep.3 = (f32[768,768]{1,0:T(8,128)}, bf16[768,768]{1,0:T(8,128)(2,1)}) custom-call(bf16[1024,3072]{1,0:T(8,128)(2,1)} %get-tuple-element.125.a_ref, bf16[1024,768]{1,0:T(8,128)(2,1)} %get-tuple-element.88.refs_0_.b_ref, bf16[2,768,768]{2,1,0:T(8,128)(2,1)} %copy-done.58), custom_call_target="tpu_custom_call" | custom-call | flops 7000000000 | bytes 14000000 | tf_op jit(solution)/shard_map/outer_keep/pallas_call | solution.py:348
  456.6 7.6 %outer_keep.2 = (f32[768,768]{1,0:T(8,128)}, bf16[768,768]{1,0:T(8,128)(2,1)}) custom-call(bf16[1024,3072]{1,0:T(8,128)(2,1)} %get-tuple-element.121.a_ref, bf16[1024,768]{1,0:T(8,128)(2,1)} %get-tuple-element.122.b_ref, bf16[2,768,768]{2,1,0:T(8,128)(2,1)} %collective-permute-done.122.add_ref), custom_call_target="tpu_custom_call" | custom-call | flops 7000000000 | bytes 14000000 | tf_op jit(solution)/shard_map/outer_keep/pallas_call | solution.py:348
  508.9 7.5 %collective-permute-done.134 = bf16[384,768]{1,0:T(8,128)(2,1)S(1)} collective-permute-done((bf16[384,768]{1,0:T(8,128)(2,1)S(1)}, bf16[384,768]{1,0:T(8,128)(2,1)S(1)}, u32[]{:S(2)}, u32[]{:S(2)}) %collective-permute-start.134) | collective-permute-done | bytes 589856 | tf_op jit(solution)/shard_map/ppermute | solution.py:519
  517.2 13.9 %collective-permute-done.76.refs_10_ = bf16[4,48,384]{2,1,0:T(8,128)(2,1)S(1)} collective-permute-done((bf16[4,48,384]{2,1,0:T(8,128)(2,1)S(1)}, bf16[4,48,384]{2,1,0:T(8,128)(2,1)S(1)}, u32[]{:S(2)}, u32[]{:S(2)}) %collective-permute-start.76) | collective-permute-done | bytes 147488 | tf_op jit(solution)/shard_map/ppermute | solution.py:519
  547.4 7.7 %collective-permute-done.136 = bf16[96,768]{1,0:T(8,128)(2,1)S(1)} collective-permute-done((bf16[96,768]{1,0:T(8,128)(2,1)S(1)}, bf16[96,768]{1,0:T(8,128)(2,1)S(1)}, u32[]{:S(2)}, u32[]{:S(2)}) %collective-permute-start.136) | collective-permute-done | bytes 147488 | tf_op jit(solution)/shard_map/ppermute | solution.py:519
  557.9 9.0 %collective-permute-done.126 = bf16[96,768]{1,0:T(8,128)(2,1)S(1)} collective-permute-done((bf16[96,768]{1,0:T(8,128)(2,1)S(1)}, bf16[96,768]{1,0:T(8,128)(2,1)S(1)}, u32[]{:S(2)}, u32[]{:S(2)}) %collective-permute-start.126) | collective-permute-done | bytes 147488 | tf_op jit(solution)/shard_map/ppermute | solution.py:519
  578.3 8.9 %grad_tokens.1 = bf16[1024,768]{1,0:T(8,128)(2,1)} custom-call(bf16[1024,384]{1,0:T(8,128)(2,1)} %get-tuple-element.95.refs_0_, bf16[1024,384]{1,0:T(8,128)(2,1)} %get-tuple-element.97.refs_1_.refs_0_, bf16[1024,384]{1,0:T(8,128)(2,1)} %get-tuple-element.99.refs_2_.refs_0_, bf16[1024,384]{1,0:T(8,128)(2,1)} %copy-done.65, bf16[1024,384]{1,0:T(8,128)(2,1)} %copy-done.64, ...), custom_call_target="tpu_custom_call" | custom-call | flops 6000000000 | bytes 12000000 | tf_op jit(solution)/shard_map/grad_tokens/pallas_call | solution.py:400
  587.9 6.6 %collective-permute-done.129 = bf16[1,96,768]{2,1,0:T(8,128)(2,1)S(1)} collective-permute-done((bf16[1,96,768]{2,1,0:T(8,128)(2,1)S(1)}, bf16[1,96,768]{2,1,0:T(8,128)(2,1)S(1)}, u32[]{:S(2)}, u32[]{:S(2)}) %collective-permute-start.129) | collective-permute-done | bytes 147488 | tf_op jit(solution)/shard_map/ppermute | solution.py:519
  598.1 6.3 place_heads.1
  616.5 7.9 %collective-permute-done.131.refs_1_ = bf16[4,96,768]{2,1,0:T(8,128)(2,1)S(1)} collective-permute-done((bf16[4,96,768]{2,1,0:T(8,128)(2,1)S(1)}, bf16[4,96,768]{2,1,0:T(8,128)(2,1)S(1)}, u32[]{:S(2)}, u32[]{:S(2)}) %collective-permute-start.131) | collective-permute-done | bytes 589856 | tf_op jit(solution)/shard_map/ppermute | solution.py:519
  (759 shorter events, 363.3 us)
Async XLA Ops:
  15.3 71.4 %collective-permute-start.46 = (bf16[384,768]{1,0:T(8,128)(2,1)S(1)}, bf16[384,768]{1,0:T(8,128)(2,1)S(1)}, u32[]{:S(2)}, u32[]{:S(2)}) collective-permute-start(bf16[384,768]{1,0:T(8,128)(2,1)S(1)} %pad_maximum_fusion.3), channel_id=1, source_target_pairs={{0,2},{1,3},{2,0},{3,1},{4,6},{5,7},{6,4},{7,5},{8,10},{9,11},{10,... | collective-permute-start | bytes 1769480 | tf_op jit(solution)/shard_map/ppermute | solution.py:519
  19.4 76.2 %collective-permute-start = (bf16[1024,768]{1,0:T(8,128)(2,1)}, bf16[1024,768]{1,0:T(8,128)(2,1)}, u32[]{:S(2)}, u32[]{:S(2)}) collective-permute-start(bf16[1024,768]{1,0:T(8,128)(2,1)} %a_own.5), channel_id=1, source_target_pairs={{0,1},{1,0},{2,3},{3,2},{4,5},{5,4},{6,7},{7,6},{8,9},{9,8},{10,11... | collective-permute-start | bytes 4718600 | tf_op jit(solution)/shard_map/ppermute | solution.py:519
  120.8 24.7 %collective-permute-start.41 = (bf16[768,768]{1,0:T(8,128)(2,1)S(1)}, bf16[768,768]{1,0:T(8,128)(2,1)S(1)}, u32[]{:S(2)}, u32[]{:S(2)}) collective-permute-start(bf16[768,768]{1,0:T(8,128)(2,1)S(1)} %copy-done.47), channel_id=1, source_target_pairs={{0,1},{1,0},{2,3},{3,2},{4,5},{5,4},{6,7},{7,6},{8,9},{9,8},{10,11... | collective-permute-start | bytes 3538952 | tf_op jit(solution)/shard_map/ppermute | solution.py:519
  120.9 25.1 %collective-permute-start.34 = (bf16[768,768]{1,0:T(8,128)(2,1)}, bf16[768,768]{1,0:T(8,128)(2,1)}, u32[]{:S(2)}, u32[]{:S(2)}) collective-permute-start(bf16[768,768]{1,0:T(8,128)(2,1)} %dynamic-slice_dynamic-update-slice_fusion.3.refs_11_.refs_6_), channel_id=1, source_target_pairs={{0,1},{1,0},{2,3},{3,2},{4,5},{5,4},{6,7},{7,6},{8,9},{9,8},{10,11... | collective-permute-start | bytes 3538952 | tf_op jit(solution)/shard_map/ppermute | solution.py:519
  135.0 38.7 %collective-permute-start.47 = (bf16[768,768]{1,0:T(8,128)(2,1)}, bf16[768,768]{1,0:T(8,128)(2,1)}, u32[]{:S(2)}, u32[]{:S(2)}) collective-permute-start(bf16[768,768]{1,0:T(8,128)(2,1)} %constant_dynamic-update-slice_fusion.11.refs_17_.refs_12_), channel_id=1, source_target_pairs={{0,1},{1,0},{2,3},{3,2},{4,5},{5,4},{6,7},{7,6},{8,9},{9,8},{10,11... | collective-permute-start | bytes 3538952 | tf_op jit(solution)/shard_map/ppermute | solution.py:519
  135.0 38.7 %collective-permute-start.40 = (bf16[768,768]{1,0:T(8,128)(2,1)}, bf16[768,768]{1,0:T(8,128)(2,1)}, u32[]{:S(2)}, u32[]{:S(2)}) collective-permute-start(bf16[768,768]{1,0:T(8,128)(2,1)} %constant_dynamic-update-slice_fusion.1.refs_13_.refs_8_), channel_id=1, source_target_pairs={{0,1},{1,0},{2,3},{3,2},{4,5},{5,4},{6,7},{7,6},{8,9},{9,8},{10,11... | collective-permute-start | bytes 3538952 | tf_op jit(solution)/shard_map/ppermute | solution.py:519
  145.0 28.7 %collective-permute-start.31 = (bf16[1024,128]{1,0:T(8,128)(2,1)}, bf16[1024,128]{1,0:T(8,128)(2,1)}, u32[]{:S(2)}, u32[]{:S(2)}) collective-permute-start(bf16[1024,128]{1,0:T(8,128)(2,1)} %get-tuple-element.86.mixed_other.refs_5_), channel_id=1, source_target_pairs={{0,1},{1,0},{2,3},{3,2},{4,5},{5,4},{6,7},{7,6},{8,9},{9,8},{10,11... | collective-permute-start | bytes 786440 | tf_op jit(solution)/shard_map/ppermute | solution.py:519
  145.5 28.2 %collective-permute-start.30 = (bf16[1024,128]{1,0:T(8,128)(2,1)}, bf16[1024,128]{1,0:T(8,128)(2,1)}, u32[]{:S(2)}, u32[]{:S(2)}) collective-permute-start(bf16[1024,128]{1,0:T(8,128)(2,1)} %get-tuple-element.85.mixed_other.refs_4_), channel_id=1, source_target_pairs={{0,1},{1,0},{2,3},{3,2},{4,5},{5,4},{6,7},{7,6},{8,9},{9,8},{10,11... | collective-permute-start | bytes 786440 | tf_op jit(solution)/shard_map/ppermute | solution.py:519
  146.0 27.7 %collective-permute-start.29 = (bf16[1024,128]{1,0:T(8,128)(2,1)}, bf16[1024,128]{1,0:T(8,128)(2,1)}, u32[]{:S(2)}, u32[]{:S(2)}) collective-permute-start(bf16[1024,128]{1,0:T(8,128)(2,1)} %get-tuple-element.84.mixed_other.refs_3_), channel_id=1, source_target_pairs={{0,1},{1,0},{2,3},{3,2},{4,5},{5,4},{6,7},{7,6},{8,9},{9,8},{10,11... | collective-permute-start | bytes 786440 | tf_op jit(solution)/shard_map/ppermute | solution.py:519
  223.3 26.5 %collective-permute-start.48 = (bf16[1024,768]{1,0:T(8,128)(2,1)}, bf16[1024,768]{1,0:T(8,128)(2,1)}, u32[]{:S(2)}, u32[]{:S(2)}) collective-permute-start(bf16[1024,768]{1,0:T(8,128)(2,1)} %get-tuple-element.93.ga_own.a_own), channel_id=1, source_target_pairs={{0,1},{1,0},{2,3},{3,2},{4,5},{5,4},{6,7},{7,6},{8,9},{9,8},{10,11... | collective-permute-start | bytes 4718600 | tf_op jit(solution)/shard_map/ppermute | solution.py:519
  248.4 64.5 %collective-permute-start.119 = (f32[10,768]{1,0:T(8,128)S(1)}, f32[10,768]{1,0:T(8,128)S(1)}, u32[]{:S(2)}, u32[]{:S(2)}) collective-permute-start(f32[10,768]{1,0:T(8,128)S(1)} %add.417), channel_id=1, source_target_pairs={{0,4},{1,5},{2,6},{3,7},{4,0},{5,1},{6,2},{7,3},{8,12},{9,13},{10,... | collective-permute-start | bytes 92168 | tf_op jit(solution)/shard_map/ppermute | solution.py:519
  326.6 120.2 %collective-permute-start.132 = (bf16[2,768,768]{2,1,0:T(8,128)(2,1)}, bf16[2,768,768]{2,1,0:T(8,128)(2,1)S(1)}, u32[]{:S(2)}, u32[]{:S(2)}) collective-permute-start(bf16[2,768,768]{2,1,0:T(8,128)(2,1)} %outer_send.3), channel_id=1, source_target_pairs={{0,1},{1,0},{2,3},{3,2},{4,5},{5,4},{6,7},{7,6},{8,9},{9,8},{10,11... | collective-permute-start | bytes 7077896 | tf_op jit(solution)/shard_map/ppermute | solution.py:519
  336.2 119.3 %collective-permute-start.122 = (bf16[2,768,768]{2,1,0:T(8,128)(2,1)}, bf16[2,768,768]{2,1,0:T(8,128)(2,1)}, u32[]{:S(2)}, u32[]{:S(2)}) collective-permute-start(bf16[2,768,768]{2,1,0:T(8,128)(2,1)} %outer_send.2), channel_id=1, source_target_pairs={{0,1},{1,0},{2,3},{3,2},{4,5},{5,4},{6,7},{7,6},{8,9},{9,8},{10,11... | collective-permute-start | bytes 7077896 | tf_op jit(solution)/shard_map/ppermute | solution.py:519
  441.1 23.1 %collective-permute-start.69 = (bf16[48,384]{1,0:T(8,128)(2,1)S(1)}, bf16[48,384]{1,0:T(8,128)(2,1)S(1)}, u32[]{:S(2)}, u32[]{:S(2)}) collective-permute-start(bf16[48,384]{1,0:T(8,128)(2,1)S(1)} %get-tuple-element.220), channel_id=1, source_target_pairs={{0,8},{1,9},{2,10},{3,11},{4,12},{5,13},{6,14},{7,15},{8,0},{9,1},... | collective-permute-start | bytes 110600 | tf_op jit(solution)/shard_map/ppermute | solution.py:519
  441.5 24.4 %collective-permute-start.70 = (bf16[48,384]{1,0:T(8,128)(2,1)S(1)}, bf16[48,384]{1,0:T(8,128)(2,1)S(1)}, u32[]{:S(2)}, u32[]{:S(2)}) collective-permute-start(bf16[48,384]{1,0:T(8,128)(2,1)S(1)} %get-tuple-element.222), channel_id=1, source_target_pairs={{0,16},{1,17},{2,18},{3,19},{4,20},{5,21},{6,22},{7,23},{8,24},{9,... | collective-permute-start | bytes 110600 | tf_op jit(solution)/shard_map/ppermute | solution.py:519
  445.5 21.9 %collective-permute-start.71 = (bf16[48,384]{1,0:T(8,128)(2,1)S(1)}, bf16[48,384]{1,0:T(8,128)(2,1)S(1)}, u32[]{:S(2)}, u32[]{:S(2)}) collective-permute-start(bf16[48,384]{1,0:T(8,128)(2,1)S(1)} %get-tuple-element.221), channel_id=1, source_target_pairs={{0,24},{1,25},{2,26},{3,27},{4,28},{5,29},{6,30},{7,31},{8,16},{9,... | collective-permute-start | bytes 110600 | tf_op jit(solution)/shard_map/ppermute | solution.py:519
  446.9 21.5 %collective-permute-start.54 = (bf16[48,384]{1,0:T(8,128)(2,1)S(1)}, bf16[48,384]{1,0:T(8,128)(2,1)S(1)}, u32[]{:S(2)}, u32[]{:S(2)}) collective-permute-start(bf16[48,384]{1,0:T(8,128)(2,1)S(1)} %get-tuple-element.223), channel_id=1, source_target_pairs={{0,8},{1,9},{2,10},{3,11},{4,12},{5,13},{6,14},{7,15},{8,0},{9,1},... | collective-permute-start | bytes 110600 | tf_op jit(solution)/shard_map/ppermute | solution.py:519
  455.6 34.0 %collective-permute-start.133 = (bf16[768,768]{1,0:T(8,128)(2,1)}, bf16[768,768]{1,0:T(8,128)(2,1)S(1)}, u32[]{:S(2)}, u32[]{:S(2)}) collective-permute-start(bf16[768,768]{1,0:T(8,128)(2,1)} %get-tuple-element.127), channel_id=1, source_target_pairs={{0,2},{1,3},{2,0},{3,1},{4,6},{5,7},{6,4},{7,5},{8,10},{9,11},{10,... | collective-permute-start | bytes 3538952 | tf_op jit(solution)/shard_map/ppermute | solution.py:519
  467.4 29.1 %collective-permute-start.123 = (bf16[768,768]{1,0:T(8,128)(2,1)}, bf16[768,768]{1,0:T(8,128)(2,1)S(1)}, u32[]{:S(2)}, u32[]{:S(2)}) collective-permute-start(bf16[768,768]{1,0:T(8,128)(2,1)} %get-tuple-element.124), channel_id=1, source_target_pairs={{0,2},{1,3},{2,0},{3,1},{4,6},{5,7},{6,4},{7,5},{8,10},{9,11},{10,... | collective-permute-start | bytes 3538952 | tf_op jit(solution)/shard_map/ppermute | solution.py:519
  497.9 33.3 %collective-permute-start.124 = (bf16[384,768]{1,0:T(8,128)(2,1)S(1)}, bf16[384,768]{1,0:T(8,128)(2,1)S(1)}, u32[]{:S(2)}, u32[]{:S(2)}) collective-permute-start(bf16[384,768]{1,0:T(8,128)(2,1)S(1)} %slice.920), channel_id=1, source_target_pairs={{0,4},{1,5},{2,6},{3,7},{4,0},{5,1},{6,2},{7,3},{8,12},{9,13},{10,... | collective-permute-start | bytes 1769480 | tf_op jit(solution)/shard_map/ppermute | solution.py:519
  506.8 33.6 %collective-permute-start.51 = (bf16[1024,384]{1,0:T(8,128)(2,1)S(1)}, bf16[1024,384]{1,0:T(8,128)(2,1)S(1)}, u32[]{:S(2)}, u32[]{:S(2)}) collective-permute-start(bf16[1024,384]{1,0:T(8,128)(2,1)S(1)} %copy-done.60), channel_id=1, source_target_pairs={{0,1},{1,0},{2,3},{3,2},{4,5},{5,4},{6,7},{7,6},{8,9},{9,8},{10,11... | collective-permute-start | bytes 2359304 | tf_op jit(solution)/shard_map/ppermute | solution.py:519
  506.9 33.7 %collective-permute-start.50 = (bf16[1024,384]{1,0:T(8,128)(2,1)S(1)}, bf16[1024,384]{1,0:T(8,128)(2,1)S(1)}, u32[]{:S(2)}, u32[]{:S(2)}) collective-permute-start(bf16[1024,384]{1,0:T(8,128)(2,1)S(1)} %copy-done.61), channel_id=1, source_target_pairs={{0,1},{1,0},{2,3},{3,2},{4,5},{5,4},{6,7},{7,6},{8,9},{9,8},{10,11... | collective-permute-start | bytes 2359304 | tf_op jit(solution)/shard_map/ppermute | solution.py:519
  508.9 33.4 %collective-permute-start.49 = (bf16[1024,384]{1,0:T(8,128)(2,1)S(1)}, bf16[1024,384]{1,0:T(8,128)(2,1)S(1)}, u32[]{:S(2)}, u32[]{:S(2)}) collective-permute-start(bf16[1024,384]{1,0:T(8,128)(2,1)S(1)} %copy-done.62), channel_id=1, source_target_pairs={{0,1},{1,0},{2,3},{3,2},{4,5},{5,4},{6,7},{7,6},{8,9},{9,8},{10,11... | collective-permute-start | bytes 2359304 | tf_op jit(solution)/shard_map/ppermute | solution.py:519
  597.1 27.2 %collective-permute-start.131 = (bf16[4,96,768]{2,1,0:T(8,128)(2,1)S(1)}, bf16[4,96,768]{2,1,0:T(8,128)(2,1)S(1)}, u32[]{:S(2)}, u32[]{:S(2)}) collective-permute-start(bf16[4,96,768]{2,1,0:T(8,128)(2,1)S(1)} %pad_maximum_fusion.4.refs_0_), channel_id=1, source_target_pairs={{0,4},{1,5},{2,6},{3,7},{4,0},{5,1},{6,2},{7,3},{8,12},{9,13},{10,... | collective-permute-start | bytes 1769480 | tf_op jit(solution)/shard_map/ppermute | solution.py:519
  (272 other events, 3246.0 us)

commit v2 on v1

v2 whole, which is shorter than its diff:
```python
import functools

import jax
import jax.numpy as jnp
from jax import lax
from jax.experimental import pallas as pl
from jax.experimental.pallas import tpu as pltpu
from jax.sharding import PartitionSpec as P

MASK_SCALE = 4.0

BF = jnp.bfloat16
F32 = jnp.float32
NT = (((1,), (1,)), ((), ()))
NN = (((1,), (0,)), ((), ()))
TN = (((0,), (0,)), ((), ()))
VMEM_LIMIT = 56 * 1024 * 1024
SIZES = (8, 4, 2, 2)

ORDER_A, ORDER_B, OWN_CORE, OTHER_CORE, PLACE = 0, 16, 32, 33, 34

COST = 0.05

def cost(us):
    return pl.CostEstimate(flops=int(us * 1.0e9 * COST), transcendentals=0, bytes_accessed=int(us * 2.0e6 * COST))

def dot(a, b, dims=NN):
    return lax.dot_general(a, b, dims, preferred_element_type=F32)

def identity(n):
    return (lax.broadcasted_iota(jnp.int32, (n, n), 0) == lax.broadcasted_iota(jnp.int32, (n, n), 1)).astype(F32).astype(BF)

def params(*sem):
    return pltpu.CompilerParams(dimension_semantics=sem or None, vmem_limit_bytes=VMEM_LIMIT)

def place_mask(order_ref, pieces, codes, bias, eye):
    rows = codes.shape[0] // 16
    for head in range(2):
        slot = 0
        for group in pieces[head * 3:head * 3 + 3]:
            for j in range(group.shape[0]):
                start = pl.multiple_of(order_ref[head * 16 + slot] * rows, rows)
                codes[pl.ds(start, rows), :] = group[j, 0]
                slot += 1
        turned = dot(eye, codes[...], NT)
        bias[head] = jnp.where(turned > 0.0, turned - 4.0, turned)

def halves(seqs, length, lane):
    half = seqs // 2
    return [pl.BlockSpec((length, lane), lambda i, s, *_: (jnp.minimum(s, half - 1), i)),
            pl.BlockSpec((length, lane), lambda i, s, *_: (jnp.maximum(s - half, 0), i))]

def mask_specs(pieces):
    return [pl.BlockSpec((p.shape[0], 1, *p.shape[2:]), lambda i, s, *_: (0, i, 0, 0)) for p in pieces]

def qkv_specs(first, length):
    def part(which):
        return pl.BlockSpec((1, length, 128), lambda i, s, *_: (which, s, first + i))
    return [part(0), part(1), part(2)]

def attend_body(order_ref, q_ref, k_ref, v_ref, *refs):
    pieces, (own_ref, other_ref, total_ref), (codes, bias) = refs[:6], refs[6:9], refs[9:]
    length = codes.shape[0]
    step, count = pl.program_id(1), pl.num_programs(1)
    @pl.when(step == 0)
    def _():
        place_mask(order_ref, pieces, codes, bias, identity(length))
    half = q_ref.shape[2] // 2
    lanes = lax.broadcasted_iota(jnp.int32, (1, 2 * half), 1)
    query, keys = q_ref[0], k_ref[0]
    values_t = v_ref[0].T
    outs = []
    for head in range(2):
        own = (lanes >= half) if head else (lanes < half)
        scores = dot(keys, jnp.where(own, query, jnp.zeros_like(query)), NT) + bias[head]
        highest = jnp.max(scores, axis=0, keepdims=True)
        powers = jnp.exp(scores - highest)
        summed = jnp.sum(powers, axis=0, keepdims=True)
        probs = (powers * (1.0 / summed)).astype(BF)
        outs.append(dot(values_t[head * half:(head + 1) * half], probs))
        total_ref[0, 0, head:head + 1, :] = highest + jnp.log(summed)
    mixed = jnp.concatenate(outs, axis=0).T.astype(BF)
    @pl.when(step < count // 2)
    def _():
        own_ref[...] = mixed
    @pl.when(step >= count // 2)
    def _():
        other_ref[...] = mixed

def attend(first, count, order, qkv, pieces):
    _, tokens, width = qkv.shape
    length = pieces[0].shape[3]
    seqs = tokens // length
    sds = jax.ShapeDtypeStruct
    return pl.pallas_call(
        attend_body,
        grid_spec=pltpu.PrefetchScalarGridSpec(
            num_scalar_prefetch=1, grid=(count, seqs),
            in_specs=qkv_specs(first, length) + mask_specs(pieces),
            out_specs=[*halves(seqs, length, 128), pl.BlockSpec((1, 1, 8, length), lambda i, s, *_: (i, s, 0, 0))],
            scratch_shapes=[pltpu.VMEM((length, length), BF), pltpu.VMEM((2, length, length), F32)],
        ),
        out_shape=[sds((tokens // 2, count * 128), BF)] * 2 + [sds((count, seqs, 8, length), F32)],
        compiler_params=params("arbitrary", "arbitrary"),
        cost_estimate=cost(9 * count),
        name="attend",
    )(order, qkv, qkv, qkv, *pieces)

def attend_back_body(groups, has_out, info_ref, *refs):
    (q_ref, k_ref, v_ref, mixed_own, mixed_other, ga_own, ga_other, wout_ref, total_ref, tok_own, tok_other), refs = refs[:11], refs[11:]
    pieces, refs = refs[:6], refs[6:]
    all_own, all_other, small_ref = (), (), None
    if has_out:
        all_own, all_other, small_ref, refs = refs[:has_out], refs[has_out:2 * has_out], refs[2 * has_out], refs[2 * has_out + 1:]
    own_ref, other_ref, refs = refs[0], refs[1], refs[2:]
    outs, refs = refs[:4 * len(groups)], refs[4 * len(groups):]
    codes, bias, acc, weight, extra = refs[:5]
    weight_out = refs[5] if has_out else None
    length = codes.shape[0]
    step, steps = pl.program_id(0), pl.num_programs(0)
    @pl.when(step == 0)
    def _():
        place_mask(info_ref, pieces, codes, bias, identity(length))
        acc[...] = jnp.zeros_like(acc)
        weight[...] = jnp.zeros_like(weight)
        extra[...] = jnp.zeros_like(extra)
        if has_out:
            extra[0:small_ref.shape[0], :] = small_ref[...]
            weight_out[...] = jnp.zeros_like(weight_out)
    half = q_ref.shape[2] // 2
    lanes = lax.broadcasted_iota(jnp.int32, (1, 2 * half), 1)
    query, keys, values = q_ref[0], k_ref[0], v_ref[0]
    keys_t = keys.T
    is_own = step < steps // 2
    grad_attn = jnp.where(is_own, ga_own[...], ga_other[...])
    grad = dot(grad_attn, wout_ref[...], NT).astype(BF)
    mixed = jnp.where(is_own, mixed_own[...], mixed_other[...])
    inner = (grad.astype(F32) * mixed.astype(F32)).T
    dq, dk, dv = [], [], []
    for head in range(2):
        own = (lanes >= half) if head else (lanes < half)
        scores = dot(keys, jnp.where(own, query, jnp.zeros_like(query)), NT) + bias[head]
        probs = jnp.exp(scores - total_ref[0, 0, head:head + 1, :])
        delta = jnp.sum(inner[head * half:(head + 1) * half], axis=0, keepdims=True)
        grad_probs = dot(values, jnp.where(own, grad, jnp.zeros_like(grad)), NT)
        grad_scores = probs * (grad_probs - delta)
        acc[head] += grad_scores
        low = grad_scores.astype(BF)
        dv.append(dot(probs.astype(BF), grad))
        dk.append(dot(low, query))
        dq.append(dot(keys_t[head * half:(head + 1) * half], low))
    first = lanes < half
    result = jnp.concatenate([(jnp.concatenate(dq, axis=0).T * 0.125).astype(BF),
                              jnp.where(first, dk[0], dk[1]).astype(BF),
                              jnp.where(first, dv[0], dv[1]).astype(BF)], axis=1)
    @pl.when(is_own)
    def _():
        own_ref[...] = result
    @pl.when(jnp.logical_not(is_own))
    def _():
        other_ref[...] = result
    weight[...] += dot(jnp.where(is_own, tok_own[...], tok_other[...]), result, TN)
    sums = jnp.sum(result.astype(F32), axis=0, keepdims=True)
    for third in range(3):
        extra[64 + third:65 + third, :] += sums[:, third * 128:(third + 1) * 128]
    if has_out:
        whole = jnp.where(is_own, jnp.concatenate([m[...] for m in all_own], axis=1),
                          jnp.concatenate([m[...] for m in all_other], axis=1))
        weight_out[...] += dot(grad_attn, whole, TN)
    rows, wrows = length // 16, weight.shape[0] // 16
    @pl.when(step == steps - 1)
    def _():
        eye = identity(length)
        for head in range(2):
            acc[head] = dot(eye, acc[head].astype(BF), NT)
        for g, (order, segments) in enumerate(groups):
            at = 16
            for out in outs[4 * g:4 * g + 4]:
                at -= out.shape[0]
                for j in range(out.shape[0]):
                    place = info_ref[order + at + j]
                    row = 0
                    for kind, k in segments:
                        if kind == "mask":
                            value = acc[k, pl.ds(pl.multiple_of(place * rows, rows), rows), :].astype(BF)
                            for t in range(length // 128):
                                out[j, row:row + rows, :] = value[:, t * 128:(t + 1) * 128]
                                row += rows
                        elif kind == "extra":
                            out[j, row:row + 16, :] = extra[pl.ds(pl.multiple_of(place * 16, 16), 16), :].astype(BF)
                            row += 16
                        else:
                            source = weight if kind == "weight" else weight_out
                            value = source[pl.ds(pl.multiple_of(place * wrows, wrows), wrows), k * 128:(k + 1) * 128]
                            out[j, row:row + wrows, :] = value.astype(BF)
                            row += wrows

def segment_rows(kind, length, width):
    return {"mask": length // 4, "extra": 16}.get(kind, width // 16)

def attend_back(pair, local, groups, info, qkv, mixed, grad_attn, w_out, total, tokens, pieces, all_mixed=(), small=None):
    _, seqs, _, length = total.shape
    rows_all, width = 2 * tokens[0].shape[0], tokens[0].shape[1]
    half = seqs // 2
    def split(wide, at=0):
        return [pl.BlockSpec((length, wide), lambda s, *_: (jnp.minimum(s, half - 1), at)),
                pl.BlockSpec((length, wide), lambda s, *_: (jnp.maximum(s - half, 0), at))]
    def part(which):
        return pl.BlockSpec((1, length, 128), lambda s, *_: (which, s, pair))
    masks = [pl.BlockSpec((p.shape[0], 1, *p.shape[2:]), lambda s, *_: (0, local, 0, 0)) for p in pieces]
    extras, extra_specs = [], []
    scratch = [pltpu.VMEM((length, length), BF), pltpu.VMEM((2, length, length), F32), pltpu.VMEM((2, length, length), F32),
               pltpu.VMEM((width, 384), F32), pltpu.VMEM((256, 128), F32)]
    if all_mixed:
        extras = [m[0] for m in all_mixed] + [m[1] for m in all_mixed] + [small]
        extra_specs = [split(m.shape[1])[k // len(all_mixed)] for k, m in enumerate(extras[:-1])] + [full(small.shape)]
        scratch.append(pltpu.VMEM((width, width // 2), F32))
    sds = jax.ShapeDtypeStruct
    shapes = [(n, sum(segment_rows(kind, length, width) for kind, _ in segments), 128) for _, segments in groups for n in SIZES]
    return pl.pallas_call(
        functools.partial(attend_back_body, groups, len(all_mixed)),
        grid_spec=pltpu.PrefetchScalarGridSpec(
            num_scalar_prefetch=1, grid=(seqs,),
            in_specs=[part(0), part(1), part(2), *split(128, local), *split(width),
                      pl.BlockSpec((128, width), lambda s, info: (info[OWN_CORE] * 3 + pair, 0)),
                      pl.BlockSpec((1, 1, 8, length), lambda s, *_: (local, s, 0, 0)), *split(width), *masks, *extra_specs],
            out_specs=split(384) + [full(x) for x in shapes],
            scratch_shapes=scratch,
        ),
        out_shape=[sds((rows_all // 2, 384), BF)] * 2 + [sds(x, BF) for x in shapes],
        compiler_params=params("arbitrary"),
        cost_estimate=cost(18 + 3 * bool(all_mixed)),
        name="attend_back",
    )(info, qkv, qkv, qkv, *mixed, *grad_attn, w_out, total, *tokens, *pieces, *extras)

def full(shape):
    return pl.BlockSpec(shape, lambda *_: (0,) * len(shape))

def project_body(info_ref, own_ref, other_ref, w_ref, shift_ref, out_ref):
    third = pl.program_id(0)
    scale = jnp.where(third == 0, 0.125, 1.0)
    rows = own_ref.shape[0]
    for i, ref in enumerate((own_ref, other_ref)):
        value = (dot(ref[...], w_ref[...]) + shift_ref[...]).astype(BF)
        out_ref[0, i * rows:(i + 1) * rows] = (value.astype(F32) * scale).astype(BF)

def project(info, own_tokens, other_tokens, w_qkv, shift):
    rows, width = own_tokens.shape
    own = width // 2
    return pl.pallas_call(
        project_body,
        grid_spec=pltpu.PrefetchScalarGridSpec(
            num_scalar_prefetch=1, grid=(3,),
            in_specs=[full((rows, width)), full((rows, width)),
                      pl.BlockSpec((width, own), lambda t, info: (0, 2 * t + info[OWN_CORE])),
                      pl.BlockSpec((1, own), lambda t, info: (0, 2 * t + info[OWN_CORE]))],
            out_specs=pl.BlockSpec((1, 2 * rows, own), lambda t, c: (t, 0, 0)),
        ),
        out_shape=jax.ShapeDtypeStruct((3, 2 * rows, own), BF),
        compiler_params=params("arbitrary"),
        cost_estimate=cost(8),
        name="project",
    )(info, own_tokens, other_tokens, w_qkv, shift)

def erf_parts(u):
    x = jnp.abs(u) * 0.7071067811865476
    t = 1.0 / (1.0 + 0.3275911 * x)
    e = jnp.exp(-0.5 * u * u)
    poly = t * (0.127414796 + t * (-0.142248368 + t * (0.7107068705 + t * (-0.7265760135 + t * 0.5307027145))))
    tail = poly * e
    return jnp.where(u < 0.0, tail, 1.0 - tail), e * 0.3989422804014327

def row_mean(v):
    return jnp.mean(v, axis=-1, keepdims=True)

def ffn_body(info_ref, *refs):
    tok_ref, gout_ref = refs[:2]
    count = len(refs) - 22
    mixed, (wout_ref, vec_ref, bin_ref), refs = refs[2:2 + count], refs[2 + count:5 + count], refs[5 + count:]
    w_in, w_down = refs[:4], refs[4:8]
    out_ref, low_ref, active_ref, slope_ref, gsec_ref, gbr_ref, norm_ref, inv_ref, sums_ref = refs[8:]
    bias_out, gain1, shift1, bias_down, gain2, shift2 = (vec_ref[i:i + 1] for i in range(6))
    value = tok_ref[...].astype(F32) + bias_out
    half = wout_ref.shape[0] // 2
    for side in range(2):
        part = jnp.concatenate([m[...] for m in mixed[side * count // 2:(side + 1) * count // 2]], axis=1)
        start = pl.multiple_of(info_ref[OWN_CORE + side] * half, half)
        value += dot(part, wout_ref[pl.ds(start, half), :])
    centered = value - row_mean(value)
    inverse = lax.rsqrt(row_mean(centered * centered) + 1e-12)
    normal = centered * inverse
    norm_ref[...] = normal
    inv_ref[...] = jnp.broadcast_to(inverse, inv_ref.shape)
    first = normal * gain1 + shift1
    low = first.astype(BF)
    low_ref[...] = low
    width = low.shape[1]
    branch = first + bias_down
    for b in range(4):
        pre = dot(low, w_in[b][...], NT) + bin_ref[b:b + 1]
        cum, dens = erf_parts(pre)
        act = (pre * cum).astype(BF)
        active_ref[b * width:(b + 1) * width, :] = act.T
        slope_ref[:, b * width:(b + 1) * width] = (cum + pre * dens).astype(slope_ref.dtype)
        branch += dot(act, w_down[b][...])
    centered = branch - row_mean(branch)
    inverse = lax.rsqrt(row_mean(centered * centered) + 1e-12)
    normal = centered * inverse
    out_ref[...] = (normal * gain2 + shift2).astype(BF)
    grad = gout_ref[...].astype(F32)
    inner = grad * gain2
    back = inverse * (inner - row_mean(inner) - normal * row_mean(inner * normal))
    gsec_ref[...] = back
    gbr_ref[...] = back.astype(BF)
    @pl.when(pl.program_id(0) == 0)
    def _():
        sums_ref[...] = jnp.zeros_like(sums_ref)
    total = lambda v: jnp.sum(v, axis=0, keepdims=True)
    sums_ref[0:1] += total(grad * normal)
    sums_ref[1:2] += total(grad)
    sums_ref[2:3] += total(back)

def ffn(info, tokens, grad_out, mixed, w_out, vecs, b_in, w_in, w_down, tile=256):
    rows, width = tokens.shape
    hidden = 4 * width
    row = lambda n: pl.BlockSpec((tile, n), lambda i, *_: (i, 0))
    sds = jax.ShapeDtypeStruct
    return pl.pallas_call(
        ffn_body,
        grid_spec=pltpu.PrefetchScalarGridSpec(num_scalar_prefetch=1, grid=(rows // tile,), in_specs=[row(width), row(width)] + [row(m.shape[1]) for m in mixed]
        + [full(a.shape) for a in (w_out, vecs, b_in, *w_in, *w_down)],
        out_specs=[row(width), row(width), pl.BlockSpec((hidden, tile), lambda i, *_: (0, i)), row(hidden), row(width), row(width), row(width), row(128),
                   full((8, width))]),
        out_shape=[sds((rows, width), BF), sds((rows, width), BF), sds((hidden, rows), BF), sds((rows, hidden), BF),
                   sds((rows, width), F32), sds((rows, width), BF), sds((rows, width), F32), sds((rows, 128), F32), sds((8, width), F32)],
        compiler_params=params("arbitrary"),
        cost_estimate=cost(30),
        name="ffn",
    )(info, tokens, grad_out, *mixed, w_out, vecs, b_in, *w_in, *w_down)

def ffn_back_body(info_ref, *refs):
    gbr_ref, slope_ref, gsec_ref, norm_ref, inv_ref, vec_ref, before_ref = refs[:7]
    w_in, w_down = refs[7:11], refs[11:15]
    gpre_ref, gone_ref, gattn_ref, small_ref, sums_ref = refs[15:]
    gain1 = vec_ref[1:2]
    @pl.when(pl.program_id(0) == 0)
    def _():
        sums_ref[...] = jnp.zeros_like(sums_ref)
    total = lambda v: jnp.sum(v, axis=0, keepdims=True)
    width = gbr_ref.shape[1]
    grad = gsec_ref[...]
    low = gbr_ref[...]
    for b in range(4):
        at = slice(b * width, (b + 1) * width)
        gpre = (dot(low, w_down[b][...], NT) * slope_ref[:, at].astype(F32)).astype(BF)
        gpre_ref[at, :] = gpre.T
        sums_ref[4 + b:5 + b] += total(gpre.astype(F32))
        grad += dot(gpre, w_in[b][...])
    normal, inverse = norm_ref[...], inv_ref[:, 0:1]
    inner = grad * gain1
    back = inverse * (inner - row_mean(inner) - normal * row_mean(inner * normal))
    gone_ref[...] = back
    gattn_ref[...] = back.astype(BF)
    sums_ref[0:1] += total(grad * normal)
    sums_ref[1:2] += total(grad)
    sums_ref[2:3] += total(back)
    @pl.when(pl.program_id(0) == pl.num_programs(0) - 1)
    def _():
        small_ref[...] = jnp.zeros_like(small_ref)
        tiles = width // 128
        for t in range(tiles):
            at = slice(t * 128, (t + 1) * 128)
            for k in range(3):
                small_ref[k * tiles + t:k * tiles + t + 1] = before_ref[k:k + 1, at]
                small_ref[(3 + k) * tiles + t:(3 + k) * tiles + t + 1] = sums_ref[k:k + 1, at]
            for k in range(4):
                small_ref[pl.ds((6 + info_ref[PLACE + k]) * tiles + t, 1), :] = sums_ref[4 + k:5 + k, at]

def ffn_back(info, grad_branch, slope, grad_second, normal, inverse, vecs, before, w_in, w_down, tile=256):
    rows, width = grad_branch.shape
    hidden = 4 * width
    row = lambda n: pl.BlockSpec((tile, n), lambda i, *_: (i, 0))
    sds = jax.ShapeDtypeStruct
    return pl.pallas_call(
        ffn_back_body,
        grid_spec=pltpu.PrefetchScalarGridSpec(num_scalar_prefetch=1, grid=(rows // tile,), in_specs=[row(width), row(hidden), row(width), row(width), row(128)] + [full(a.shape) for a in (vecs, before, *w_in, *w_down)],
        out_specs=[pl.BlockSpec((hidden, tile), lambda i, *_: (0, i)), row(width), row(width), full((64, 128))],
            scratch_shapes=[pltpu.VMEM((8, width), F32)]),
        out_shape=[sds((hidden, rows), BF), sds((rows, width), F32), sds((rows, width), BF), sds((64, 128), F32)],
        compiler_params=params("arbitrary"),
        cost_estimate=cost(18),
        name="ffn_back",
    )(info, grad_branch, slope, grad_second, normal, inverse, vecs, before, *w_in, *w_down)

def outer_send_body(a_ref, b_ref, out_ref):
    out_ref[0] = dot(a_ref[...], b_ref[...]).astype(BF)

def outer_send(a, b):
    rows, width = b.shape
    return pl.pallas_call(
        outer_send_body,
        grid=(2,),
        in_specs=[pl.BlockSpec((width, rows), lambda i: (2 * i + 1, 0)), full((rows, width))],
        out_specs=pl.BlockSpec((1, width, width), lambda i: (i, 0, 0)),
        out_shape=jax.ShapeDtypeStruct((2, width, width), BF),
        compiler_params=params("arbitrary"),
        cost_estimate=cost(6),
        name="outer_send",
    )(a, b)

def outer_keep_body(a_ref, b_ref, add_ref, keep_ref, send_ref):
    value = dot(a_ref[...], b_ref[...]) + add_ref[0].astype(F32)
    @pl.when(pl.program_id(0) == 0)
    def _():
        send_ref[...] = value.astype(BF)
    @pl.when(pl.program_id(0) == 1)
    def _():
        keep_ref[...] = value

def outer_keep(a, b, add):
    rows, width = b.shape
    return pl.pallas_call(
        outer_keep_body,
        grid=(2,),
        in_specs=[pl.BlockSpec((width, rows), lambda i: (2 - 2 * i, 0)), full((rows, width)),
                  pl.BlockSpec((1, width, width), lambda i: (1 - i, 0, 0))],
        out_specs=[full((width, width)), full((width, width))],
        out_shape=[jax.ShapeDtypeStruct((width, width), F32), jax.ShapeDtypeStruct((width, width), BF)],
        compiler_params=params("arbitrary"),
        cost_estimate=cost(7),
        name="outer_keep",
    )(a, b, add)

def grad_tokens_body(info_ref, *refs):
    pieces, (one_ref, w_ref, out_ref, sides) = refs[:-4], refs[-4:]
    width = one_ref.shape[1]
    @pl.when(pl.program_id(0) == 0)
    def _():
        for side in range(2):
            for pair in range(3):
                for third in range(3):
                    start = pl.multiple_of(third * width + (info_ref[OWN_CORE + side] * 3 + pair) * 128, 128)
                    at = ((side * 3 + pair) * 3 + third) * 128
                    sides[:, at:at + 128] = w_ref[:, pl.ds(start, 128)]
    wide = jnp.concatenate([r[...] for r in pieces], axis=1)
    out_ref[...] = (one_ref[...] + dot(wide, sides[...], NT)).astype(BF)

def grad_tokens(info, pieces, grad_one, w, tile=256):
    rows, width = grad_one.shape
    row = lambda n: pl.BlockSpec((tile, n), lambda i, *_: (i, 0))
    return pl.pallas_call(
        grad_tokens_body,
        grid_spec=pltpu.PrefetchScalarGridSpec(
            num_scalar_prefetch=1, grid=(rows // tile,),
            in_specs=[row(p.shape[1]) for p in pieces] + [row(width), full(w.shape)],
            out_specs=row(width),
            scratch_shapes=[pltpu.VMEM(w.shape, BF)]),
        out_shape=jax.ShapeDtypeStruct((rows, width), BF),
        compiler_params=params("arbitrary"),
        cost_estimate=cost(9),
        name="grad_tokens",
    )(info, *pieces, grad_one, w)

def place_pair_body(order_of, extra_at, aliased, info_ref, *refs):
    refs = refs[aliased:]
    count = 1 + max(piece for piece, _, _ in order_of)
    sides, out_ref, extras = (refs[:count], refs[count:2 * count]), refs[2 * count], refs[2 * count + 1:]
    rows = out_ref.shape[0] // 16
    for side in range(2):
        for third, (piece, order, first) in enumerate(order_of):
            @pl.when(pl.program_id(0) == side * 3 + third)
            def _(side=side, piece=piece, order=order, first=first):
                for slot in range(16):
                    start = pl.multiple_of(info_ref[order + slot] * rows, rows)
                    out_ref[pl.ds(start, rows), :] = sides[side][piece][slot, first:first + rows, :].astype(F32)
    @pl.when(pl.program_id(0) == 0)
    def _():
        piece, order, first = extra_at
        for side in range(2):
            for slot in range(16):
                start = pl.multiple_of(info_ref[order + slot] * 16, 16)
                extras[side][pl.ds(start, 16), :] = sides[side][piece][slot, first:first + 16, :].astype(F32)

def place_pair(pair, order_of, extra_at, info, width, own, other, whole=None):
    sds = jax.ShapeDtypeStruct
    aliased = int(whole is not None)
    return pl.pallas_call(
        functools.partial(place_pair_body, order_of, extra_at, aliased),
        grid_spec=pltpu.PrefetchScalarGridSpec(
            num_scalar_prefetch=1, grid=(6,),
            in_specs=[pl.BlockSpec(memory_space=pl.ANY)] * aliased + [full(p.shape) for p in (*own, *other)],
            out_specs=[pl.BlockSpec((width, 128), lambda i, info: (0, i % 3 * (width // 128) + info[OWN_CORE + i // 3] * 3 + pair)),
                       full((256, 128)), full((256, 128))]),
        out_shape=[sds((width, 3 * width), F32), sds((256, 128), F32), sds((256, 128), F32)],
        input_output_aliases={1: 0} if aliased else {},
        compiler_params=params("arbitrary"),
        cost_estimate=cost(3),
        name="place_pair",
    )(info, *([whole] if aliased else []), *own, *other)

def place_turned_body(order, first, info_ref, own_ref, other_ref, out_ref, acc):
    width, wide = acc.shape
    rows = width // 16
    for side, piece in enumerate((own_ref, other_ref)):
        for slot in range(16):
            start = pl.multiple_of(info_ref[order + slot] * rows, rows)
            for t in range(3):
                at = first + t * rows
                acc[pl.ds(start, rows), t * 128:(t + 1) * 128] = piece[slot, at:at + rows, :].astype(F32)
        start = pl.multiple_of(info_ref[OWN_CORE + side] * wide, wide)
        out_ref[pl.ds(start, wide), :] = acc[...].T

def place_turned(order, first, info, width, own, other):
    return pl.pallas_call(
        functools.partial(place_turned_body, order, first),
        grid_spec=pltpu.PrefetchScalarGridSpec(
            num_scalar_prefetch=1, grid=(1,), in_specs=[full(own.shape), full(other.shape)], out_specs=full((width, width)),
            scratch_shapes=[pltpu.VMEM((width, width // 2), F32)]),
        out_shape=jax.ShapeDtypeStruct((width, width), F32),
        compiler_params=params("arbitrary"),
        cost_estimate=cost(4),
        name="place_turned",
    )(info, own, other)


AXES = ("dp", "mp")
CORE, ROW, COLUMN, NEAR_DEPTH, FAR_DEPTH = 1, 2, 4, 8, 16
PARTS = ((0, 1), (1, 2))
WEIGHT = [("weight", k) for k in range(3)]
MASKS = [("mask", 0), ("mask", 1)]
OUT = [("out", k) for k in range(3)]
STEPS = ((1, ORDER_B, [*MASKS, *WEIGHT, *OUT, ("extra", 0)]), (2, ORDER_B, [*MASKS, *WEIGHT, ("extra", 0)]),
         (0, ORDER_A, [*MASKS, *WEIGHT, ("extra", 0)]))


class Order:
    def __init__(self):
        self.last = None

    def hold(self, value):
        return value if self.last is None else lax.optimization_barrier((value, self.last))[0]

    def do(self, step, *operands):
        result = step(*self.hold(operands))
        self.last = jax.tree.leaves(result)[0]
        return result


class Links:
    def __init__(self, dp, mp):
        self.dp, self.mp = dp, mp
        self.direct = dp == 8 and mp == 4
        self.at_dp, self.at_mp = lax.axis_index("dp"), lax.axis_index("mp")
        self.core, self.row, self.column = self.at_mp % 2, self.at_mp // 2, self.at_dp % 2
        self.near_deep, self.far_deep = self.at_dp // 2 % 2, self.at_dp // 4
        slot = jnp.arange(16)
        z, low, high = (((slot >> 1) & 1) << 1) | ((slot & 1) << 2), (slot >> 2) & 1, slot >> 3
        if self.direct:
            def chip(x, y):
                return (self.at_dp ^ (x | z)) * 2 + (self.row ^ y)
            orders = [chip(low, high), chip(high, low)]
        else:
            orders = [slot, slot]
        rest = jnp.stack([self.core, 1 - self.core, *(self.at_mp ^ k for k in range(4))])
        self.info = jnp.concatenate([*orders, rest]).astype(jnp.int32)

    def swap(self, value, bits):
        count = self.dp * self.mp
        return lax.ppermute(value, AXES, [(i, i ^ bits) for i in range(count)])

    def grow(self, value, *axes):
        for bits in axes:
            value = jnp.concatenate([value, self.swap(value, bits)])
        return value


def pick(index, first, second):
    return jnp.where(index == 0, first, second)


def in_order(index, own, other, axis=0):
    return pick(index, jnp.stack([own, other], axis), jnp.stack([other, own], axis))


def at(value, index, axis):
    return lax.dynamic_index_in_dim(value, index, axis, False)


def axes_of(order):
    return (ROW, COLUMN) if order == ORDER_A else (COLUMN, ROW)


def add(*values):
    return sum(v.astype(F32) for v in values)


def any_hidden(links, keep, near):
    zero = jnp.zeros_like(keep)
    blocks = jnp.stack([keep, zero, near.astype(F32), zero])
    blocks = jnp.stack([blocks[links.at_mp ^ k] for k in range(4)])
    return lax.psum(lax.psum_scatter(blocks, "mp", scatter_dimension=0, tiled=False), "dp")


class Hidden:
    def __init__(self, links, order, keep, near):
        self.links, self.order, self.shape = links, order, keep.shape
        self.parts = (2, 2, 2, keep.shape[0] // 8, keep.shape[1])
        self.total, self.came = keep, links.swap(near, ROW)

    def halve(self, index, axis, bits):
        def step(total, came):
            total = total.reshape(self.parts[-axis - 3:]) + came.reshape(self.parts[-axis - 3:]).astype(F32)
            return at(total, 1 - index, axis).astype(BF), at(total, index, axis)
        away, self.total = self.order.do(step, self.total, self.came)
        self.came = self.links.swap(away, bits)

    def column(self):
        self.halve(self.links.column, 2, COLUMN)

    def near_deep(self):
        self.halve(self.links.near_deep, 1, NEAR_DEPTH)

    def far_deep(self):
        self.halve(self.links.far_deep, 0, FAR_DEPTH)

    def spread_far(self):
        self.total = self.order.do(lambda a, b: add(a, b).astype(BF), self.total, self.came)
        self.came = self.links.swap(self.total, FAR_DEPTH)

    def spread(self, index, axis, bits):
        self.total = self.order.do(lambda a, b: in_order(index, a, b, axis), self.total, self.came)
        self.came = self.links.swap(self.total, bits)

    def spread_near(self):
        self.spread(self.links.far_deep, 0, NEAR_DEPTH)

    def spread_column(self):
        self.spread(self.links.near_deep, 1, COLUMN)

    def whole(self):
        self.result = self.order.do(lambda a, b: in_order(self.links.column, a, b, 2).astype(F32).reshape(self.shape), self.total, self.came)


class Slots:
    def __init__(self, links, order, axes, masks):
        self.links, self.order, self.axes, self.masks = links, order, axes, masks
        self.slots, self.came = [], []

    def far(self, slots):
        self.slots.append(slots)
        self.came.append(self.links.swap(slots[0], self.axes[0]))

    def near(self):
        def step(mids, came):
            return jnp.concatenate([add(m, c[4:]).astype(BF) for m, c in zip(mids, came)], axis=1)
        self.beside = self.links.swap(self.order.do(step, [s[1] for s in self.slots], self.came), self.axes[1])

    def deep(self, which, first, last):
        slots, came, beside = which
        return jnp.concatenate([add(s, c[first:last]) for s, c in zip(slots, came)], axis=1) + beside[first:last].astype(F32)

    def near_deep(self):
        step = lambda *which: self.deep(which, 2, 4).astype(BF)
        sent = self.order.do(step, [s[2] for s in self.slots], self.came, self.beside)
        self.behind = self.links.swap(sent, NEAR_DEPTH)

    def far_deep(self):
        def step(which, behind):
            total = self.deep(which, 0, 2) + behind.astype(F32)
            return total[1].astype(BF), total[0]
        sent, self.total = self.order.do(step, ([s[3] for s in self.slots], self.came, self.beside), self.behind)
        self.came = self.links.swap(sent, FAR_DEPTH)

    def spread_far(self):
        def step(total, came):
            total = total + came.astype(F32)
            row, masks, rest = 0, [], []
            for slots, count in zip(self.slots, self.masks):
                rows = slots[0].shape[1]
                masks.append(total[row:row + count])
                rest.append(total[row + count:row + rows])
                row += rows
            return jnp.concatenate(rest)[None].astype(BF), masks
        self.whole, self.mask_rows = self.order.do(step, self.total, self.came)
        self.came = self.links.swap(self.whole, FAR_DEPTH)

    def spread(self, bits):
        self.whole = self.order.do(lambda a, b: jnp.concatenate([a, b]), self.whole, self.came)
        self.came = self.links.swap(self.whole, bits)


def body(dp, mp, tokens, w_qkv, bias_q, bias_v, w_out, bias_out, norm1_gain, norm1_bias, w_in, bias_in, w_down, bias_down,
         norm2_gain, norm2_bias, mask_logits, mask_noise, grad_out):
    width = w_out.shape[0]
    heads, rows_own, length = mask_logits.shape
    half = heads // 2
    links, order = Links(dp, mp), Order()
    core, info, swap, do = links.core, links.info, links.swap, order.do
    wide = lambda v: v.astype(F32)

    def chances(logits, noise):
        fraction = noise.astype(F32) / 65536.0
        return logits + jnp.log(fraction) - jnp.log(1.0 - fraction)

    def codes(logits, noise):
        logit = chances(logits, noise)
        tail = jax.nn.sigmoid(-jnp.abs(logit)) * MASK_SCALE
        return jnp.where(logit < 0.0, tail, -tail).astype(BF)

    shift = jnp.concatenate([wide(bias_q), jnp.zeros((width,), F32), wide(bias_v)])[None]
    vecs = jnp.stack([wide(v) for v in (bias_out, norm1_gain, norm1_bias, bias_down, norm2_gain, norm2_bias)]
                     + [jnp.zeros((width,), F32)] * 2)
    mixed, totals, came = [], [], []

    def attention(part, pieces):
        own, other, total = do(lambda q, m: attend(*PARTS[part], info, q, m), qkv, pieces)
        mixed.append((own, other))
        came.append(swap(other, CORE))
        totals.append(total)

    if links.direct:
        plane = (1, rows_own, length)

        def two_sides(logits, noise, bias):
            code = codes(logits, noise)
            row = jnp.pad(bias, (0, rows_own * length - bias.shape[0])).reshape(plane)
            return jnp.concatenate([pick(core, code[half:], code[:half]), row]), pick(core, code[:half], code[half:])
        away, keep = do(two_sides, mask_logits, mask_noise, bias_in)
        beside = swap(away, CORE)
        other_tokens = swap(tokens, CORE)

        def chip_codes(keep, beside):
            chip = in_order(core, keep, beside[:half], 1).reshape(half // 2, 2, 2 * rows_own, length)
            return chip.transpose(1, 0, 2, 3)[None], beside[half].reshape(-1)[:bias_in.shape[0]]
        chip, near_bias = do(chip_codes, keep, beside)
        behind = swap(chip, FAR_DEPTH)
        eighth = w_in.shape[0] // 8
        split = lambda w: w.reshape(4, 2, eighth, width)

        def to_row(w_in, w_down, *biases):
            parts = [at(at(split(w), links.at_dp // 2, 0), links.column, 0) for w in (w_in, w_down)]
            return jnp.concatenate([*parts, jnp.pad(jnp.stack(biases), ((0, 14), (0, 0)))]), at(split(w_down), 1 - links.column, 1)
        piece, straight = do(to_row, w_in, w_down, bias_in, near_bias)
        piece, straight = swap(piece, ROW), swap(straight, ROW)
        qkv = do(lambda *v: project(info, *v), tokens, other_tokens, w_qkv, shift)
        axes = ((COLUMN, ROW), (ROW, COLUMN))
        groups, seconds, fars = [None] * 2, [None] * 2, [None] * 2

        def gather_near(part):
            groups[part] = do(lambda a, b: [jnp.concatenate([a[:, h], b[:, h]]) for h in range(2)], *deep[part])
            seconds[part] = [swap(groups[part][h], axes[h][0]) for h in range(2)]

        def gather_far(part):
            both = do(lambda g, s: [jnp.concatenate(v) for v in zip(g, s)], groups[part], seconds[part])
            fars[part] = [swap(both[h], axes[h][1]) for h in range(2)]

        pairs = do(lambda a, b: [jnp.concatenate([a[:, :, p:p + n], b[:, :, p:p + n]]) for p, n in PARTS], chip, behind)
        deep = [(v, swap(v, NEAR_DEPTH)) for v in pairs]
        gather_near(0)
        piece = order.hold(piece)
        across_bias = list(piece[2 * eighth:2 * eighth + 2])
        piece = piece[:2 * eighth]
        behind = swap(piece, FAR_DEPTH)
        gather_far(0)
        gather_near(1)
        pieces = [None] * 2
        pieces[0] = [v for h in range(2) for v in (groups[0][h], seconds[0][h], fars[0][h])]
        attention(0, pieces[0])
        gather_far(1)
        pair = do(lambda a, b: in_order(links.far_deep, a, b), piece, behind)
        behind = swap(pair, NEAR_DEPTH)
        near_in, near_down = (swap(order.hold(w), CORE) for w in (w_in, w_down))
        group = do(lambda a, b: [v.reshape(4, eighth, width) for v in jnp.split(in_order(links.near_deep, a, b, 1), 2, axis=2)], pair, behind)
        around = swap(group[0], COLUMN)
        across_down = do(lambda a, b: in_order(links.column, a, b, 1).reshape(w_in.shape), group[1], straight)
        far_down = swap(across_down, CORE)
        pieces[1] = [v for h in range(2) for v in (groups[1][h], seconds[1][h], fars[1][h])]
        attention(1, pieces[1])
        across_in = do(lambda a, b: in_order(links.column, a, b, 1).reshape(w_in.shape), group[0], around)
        blocks_in = [w_in, near_in, across_in, swap(across_in, CORE)]
        blocks_down = [w_down, near_down, across_down, far_down]
        blocks_bias = [bias_in, near_bias, *across_bias]
    else:
        other_tokens = swap(tokens, CORE)
        qkv = project(info, tokens, other_tokens, w_qkv, shift)
        whole = lax.all_gather(codes(mask_logits, mask_noise), AXES, axis=1, tiled=True)
        own = lax.dynamic_slice_in_dim(whole, core * half, half, 0).reshape(half // 2, 2, 16, length // 16, length)
        own = own.transpose(1, 2, 0, 3, 4)
        pieces = [[own[h, a:b, p:p + n] for h in range(2) for a, b in ((0, 4), (4, 8), (8, 16))] for p, n in PARTS]
        attention(0, pieces[0])
        attention(1, pieces[1])
        blocks_in, blocks_down, blocks_bias = ([v[links.at_mp ^ k] for k in range(4)]
                                               for v in (lax.all_gather(w, "mp") for w in (w_in, w_down, bias_in)))
    biases = wide(jnp.stack(blocks_bias))
    out, first_low, active, slope, grad_second, grad_branch, normal, inverse, sums = do(
        lambda *v: ffn(info, *v), tokens, grad_out, [own for own, _ in mixed] + came, w_out, vecs, biases, blocks_in, blocks_down)
    sent_down = do(outer_send, active, grad_branch)
    grad_pre, grad_one, grad_attn, small = do(lambda *v: ffn_back(info, *v), grad_branch, slope, grad_second, normal, inverse, vecs,
                                              sums, blocks_in, blocks_down)
    other_attn = swap(grad_attn, CORE)
    keep_down = do(lambda *v: outer_keep(*v)[::-1], active, grad_branch, swap(sent_down, CORE))
    if links.direct:
        down = Hidden(links, order, keep_down[1], keep_down[0])
    sent_in = do(outer_send, grad_pre, first_low)
    d_own, d_other, slots = [None] * 3, [None] * 3, []

    def back(step):
        pair, place, segments = STEPS[step]
        part = min(pair, 1)
        local = pair - PARTS[part][0]
        own, other, *outs = do(
            lambda *v: attend_back(pair, local, [(place, segments)], info, *v), qkv, mixed[part], (grad_attn, other_attn), w_out,
            totals[part], (tokens, other_tokens), pieces[part], () if step else mixed, small)
        slots.append(outs)
        if links.direct:
            chains[step].far(outs)
        d_own[pair] = own
        d_other[pair] = swap(other, CORE)

    masks = [sum(kind == "mask" for kind, _ in segments) * length // 4 for _, _, segments in STEPS]
    chains = [Slots(links, order, axes_of(place), [count]) for (_, place, _), count in zip(STEPS, masks)]
    back(0)
    if links.direct:
        down.column()
    keep_in = do(lambda *v: outer_keep(*v)[::-1], grad_pre, first_low, swap(sent_in, CORE))
    if links.direct:
        inside = Hidden(links, order, keep_in[1], keep_in[0])
    back(1)
    if links.direct:
        zero, one, two = chains
        down.near_deep()
        zero.near()
    back(2)
    if links.direct:
        near, far = COLUMN, ROW
        for chain, step in (
            (inside, "column"), (down, "far_deep"), (zero, "near_deep"), (one, "near"), (None, "tokens"),
            (inside, "near_deep"), (two, "near"), (zero, "far_deep"), (down, "spread_far"), (one, "near_deep"),
            (inside, "far_deep"), (two, "near_deep"), (zero, "spread_far"), (down, "spread_near"), (one, "far_deep"),
            (inside, "spread_far"), (two, "far_deep"), (zero, NEAR_DEPTH), (down, "spread_column"), (one, "spread_far"),
            (inside, "spread_near"), (two, "spread_far"), (zero, near), (one, NEAR_DEPTH),
            (inside, "spread_column"), (two, NEAR_DEPTH), (down, "whole"), (zero, far), (one, near),
            (two, near), (inside, "whole"), (zero, CORE), (one, far), (two, far), (one, CORE), (two, CORE),
        ):
            if step == "tokens":
                grad_in = do(lambda *v: grad_tokens(info, *v), [*d_own, *d_other], grad_one, w_qkv)
            elif isinstance(step, int):
                chain.spread(step)
            else:
                getattr(chain, step)()
        grad_w_down, grad_w_in = down.result, inside.result
        placed = [(chain.whole, chain.came) for chain in chains]
        mask_rows = [chain.mask_rows[0].reshape(2, 4, length // 16, 128) for chain in chains]
    else:
        grad_w_down, grad_w_in = any_hidden(links, *keep_down[::-1]), any_hidden(links, *keep_in[::-1])
        grad_in = grad_tokens(info, [*d_own, *d_other], grad_one, w_qkv)
        placed, mask_rows = [], []
        for s, count in zip(slots, masks):
            own = wide(jnp.concatenate(s[::-1]))
            both = lax.psum(in_order(core, own, jnp.zeros_like(own)), AXES)
            sides = [both[core], both[1 - core]]
            placed.append([v[:, count:] for v in sides])
            mask_rows.append(jnp.stack([v[:, :count].reshape(16, 2, 4, length // 16, 128).transpose(1, 2, 0, 3, 4) for v in sides]))
    grad_w_qkv = grad_w_out = small = None
    bias, by_pair = [None] * 3, [None] * 3
    for step, (pair, _, segments) in enumerate(STEPS):
        found, row = {}, 0
        for kind, k in segments:
            if kind != "mask":
                found[kind, k] = (0, ORDER_A, row)
                row += segment_rows(kind, length, width)
        own, other = placed[step]
        if step == 0:
            grad_w_out = do(lambda *v: place_turned(ORDER_A, found["out", 0][2], info, width, *v), own, other)
        grad_w_qkv, *extras = do(
            lambda a, b, *w: place_pair(pair, [found["weight", k] for k in range(3)], found["extra", 0], info, width, [a], [b], *w),
            own, other, *([grad_w_qkv] if step else []))
        if step == 0:
            small = (extras[0][:60] + extras[1][:60]).reshape(10, width)
        bias[pair] = jnp.stack([e[64:67] for e in extras])
        by_pair[pair] = mask_rows[step]
    bias = jnp.stack(bias, axis=2)
    bias = pick(core, bias, bias[::-1]).transpose(1, 0, 2, 3).reshape(3, width)
    if links.direct:
        mask_sum = jnp.stack(by_pair).transpose(0, 1, 3, 2, 4).reshape(half, 2 * rows_own, length)
        mine = pick(core, mask_sum[:, :rows_own], mask_sum[:, rows_own:])
        theirs = swap(pick(core, mask_sum[:, rows_own:], mask_sum[:, :rows_own]), CORE)
    else:
        mine, theirs = jnp.stack(by_pair, axis=1).transpose(0, 1, 2, 4, 5, 3, 6).reshape(2, half, length, length)
        place = (links.at_dp * mp + links.at_mp) * rows_own
        mine, theirs = (lax.dynamic_slice_in_dim(m, place, rows_own, 1) for m in (mine, theirs))
    mask_sum = pick(core, jnp.concatenate([mine, theirs]), jnp.concatenate([theirs, mine]))
    mask_own = jax.nn.sigmoid(chances(mask_logits, mask_noise))
    grad_mask_logits = mask_sum * (MASK_SCALE * mask_own * (1.0 - mask_own))
    return (out, grad_in, grad_w_qkv, bias[0], bias[2], grad_w_out, small[5], small[3], small[4], grad_w_in, small[6 + links.at_mp],
            grad_w_down, small[2], small[0], small[1], grad_mask_logits)


def solution(mesh):
    both, none = ("dp", "mp"), P()
    rows, mask, split = P(both, None), P(None, both, None), P("mp", None)
    ins = (rows, none, none, none, none, none, none, none, split, P("mp"), split, none, none, none, mask, mask, rows)
    outs = (rows, rows, none, none, none, none, none, none, none, split, P("mp"), split, none, none, none, mask)
    step = functools.partial(body, mesh.shape["dp"], mesh.shape["mp"])
    return jax.shard_map(step, mesh=mesh, in_specs=ins, out_specs=outs, check_vma=False)
```

time: 635 us -> 449 us (0.71)
  starting transfers between devices: 179 us -> 66.6 us
  waiting for transfers between devices: 146 us -> 89.6 us
  between operations: 23.7 us -> 2.62 us
  other arithmetic: 14.3 us -> 26.9 us
    ppermute x173 -> x72, starting transfers between devices: 179 us -> 66.6 us  [swap(): return lax.ppermute(value, AXES, [(i, i ^ bits) for i in range(count)])]
    ppermute x173 -> x72, waiting for transfers between devices: 146 us -> 89.6 us  [swap(): return lax.ppermute(value, AXES, [(i, i ^ bits) for i in range(count)])]
    optimization_barrier x0 -> x18, local copies, waits for them, and re-layouts: none -> 17.1 us  [hold(): lax.optimization_barrier((value, self.last))[0]]
    unnamed x269 -> x142, local copies, waits for them, and re-layouts: 29.1 us -> 14 us
    add x13 -> x14, other arithmetic: 1.05 us -> 8.67 us  [the longest x6 5.45 us: step(): total.reshape(self.parts[-axis - 3:])]
    slice x24 -> x11, local copies, waits for them, and re-layouts: 7.19 us -> 0.08 us  [the longest x4 0.03 us: step(): masks.append(total[row:row + count])]
    convert_element_type x12 -> x11, other arithmetic: 1.22 us -> 7.93 us  [the longest x3 2.93 us: near_deep(): step = lambda *which: self.deep(which, 2, 4).astype(BF)]
    dynamic_slice x7 -> x1, local copies, waits for them, and re-layouts: 7.02 us -> 0.61 us  [body(): small[6 + links.at_mp]]
  transfers between devices with their start and end apart: 173 -> 72, of which waited for: 61 -> 26; matrix products, arithmetic and copies ran while one was open for 10% -> 15% of each run, Pallas kernels for 24% -> 35%
where the time goes in v2:
time: 449 us; the launch traced here: 441 us
  Pallas kernels  199 us (44%)
  waiting for transfers between devices  89.6 us (20%)
  starting transfers between devices  66.6 us (15%)
  local copies, waits for them, and re-layouts  56.4 us (13%)
  other arithmetic  26.9 us (6%)
    ppermute x72, waiting for transfers between devices, swap(): return lax.ppermute(value, AXES, [(i, i ^ bits) for i in range(count)])  89.6 us
    ppermute x72, starting transfers between devices, swap(): return lax.ppermute(value, AXES, [(i, i ^ bits) for i in range(count)])  66.6 us
    pallas_call x3, Pallas kernels, attend_back(): pl.pallas_call(functools.partial(attend_back_body, groups, len(all_mixed)...  54.7 us
    pallas_call x1, Pallas kernels, ffn(): pl.pallas_call(ffn_body, grid_spec=pltpu.PrefetchScalarGridSpec(num_scala...  33.9 us
    pallas_call x2, Pallas kernels, attend(): pl.pallas_call(attend_body, grid_spec=pltpu.PrefetchScalarGridSpec(num_sc...  25.3 us
    pallas_call x1, Pallas kernels, ffn_back(): pl.pallas_call(ffn_back_body, grid_spec=pltpu.PrefetchScalarGridSpec(num_...  20.2 us
    optimization_barrier x18, local copies, waits for them, and re-layouts, hold(): lax.optimization_barrier((value, self.last))[0]  17.1 us
    pallas_call x3, Pallas kernels, place_pair(): pl.pallas_call(functools.partial(place_pair_body, order_of, extra_at, ali...  14.4 us
  transfers between devices with their start and end apart: 72, of which 26 were waited for; matrix products, arithmetic and copies ran while one was open for 15% of the time, Pallas kernels for 35%

profile of v2, /device:TPU:0, one launch (start us, length us, event | category | flops | bytes accessed | tf_op | source)
XLA Modules:
  0.0 440.9 jit_solution(14563444715360427532)
XLA Ops:
  11.3 9.4 %project.1.q_ref.k_ref.v_ref.refs_0_.refs_1_.refs_2_ = bf16[3,2048,384]{2,1,0:T(8,128)(2,1)} custom-call(s32[38]{0:T(128)} %concatenate.84.info_ref.order_ref, bf16[1024,768]{1,0:T(8,128)(2,1)} %refs_9_.3, bf16[1024,768]{1,0:T(8,128)(2,1)} %copy-done, bf16[768,2304]{1,0:T(8,128)(2,1)} %refs_7_.4, f32[1,2304]{1,0:T(1,128)} %broadcast_in_dim.13.shift_ref), custom_call_target="tpu_custom_call" | custom-call | flops 400000000 | bytes 800000 | tf_op jit(solution)/shard_map/project/pallas_call | solution.py:250
  47.5 9.3 %attend.2 = (bf16[1024,128]{1,0:T(8,128)(2,1)}, bf16[1024,128]{1,0:T(8,128)(2,1)}, f32[1,4,8,512]{3,2,1,0:T(8,128)}) custom-call(s32[38]{0:T(128)} %concatenate.84.info_ref.order_ref, bf16[3,2048,384]{2,1,0:T(8,128)(2,1)} %project.1.q_ref.k_ref.v_ref.refs_0_.refs_1_.refs_2_, bf16[3,2048,384]{2,1,0:T(8,128)(2,1)} %project.1.q_ref.k_ref.v_ref.refs_0_.refs_1_.refs_2_, ...), custom_call_target="tpu_custom_call" | custom-call | flops 450000000 | bytes 900000 | tf_op jit(solution)/shard_map/attend/pallas_call | solution.py:95
  88.7 16.0 %attend.3 = (bf16[1024,256]{1,0:T(8,128)(2,1)}, bf16[1024,256]{1,0:T(8,128)(2,1)}, f32[2,4,8,512]{3,2,1,0:T(8,128)}) custom-call(s32[38]{0:T(128)} %concatenate.84.info_ref.order_ref, bf16[3,2048,384]{2,1,0:T(8,128)(2,1)} %project.1.q_ref.k_ref.v_ref.refs_0_.refs_1_.refs_2_, bf16[3,2048,384]{2,1,0:T(8,128)(2,1)} %project.1.q_ref.k_ref.v_ref.refs_0_.refs_1_.refs_2_, ...), custom_call_target="tpu_custom_call" | custom-call | flops 900000000 | bytes 1800000 | tf_op jit(solution)/shard_map/attend/pallas_call | solution.py:95
  117.8 33.9 %ffn.1 = (bf16[1024,768]{1,0:T(8,128)(2,1)}, bf16[1024,768]{1,0:T(8,128)(2,1)}, bf16[3072,1024]{1,0:T(8,128)(2,1)}, bf16[1024,3072]{1,0:T(8,128)(2,1)}, f32[1024...) custom-call(s32[38]{0:T(128)} %concatenate.84.info_ref.order_ref, ...), custom_call_target="tpu_custom_call" | custom-call | flops 1500000000 | bytes 3000000 | tf_op jit(solution)/shard_map/ffn/pallas_call | solution.py:328
  151.7 5.7 %outer_send.2 = bf16[2,768,768]{2,1,0:T(8,128)(2,1)} custom-call(bf16[3072,1024]{1,0:T(8,128)(2,1)} %get-tuple-element.411.a_ref, bf16[1024,768]{1,0:T(8,128)(2,1)} %get-tuple-element.412.b_ref.refs_0_), custom_call_target="tpu_custom_call" | custom-call | flops 300000000 | bytes 600000 | tf_op jit(solution)/shard_map/outer_send/pallas_call | solution.py:400
  157.8 20.2 %ffn_back.1 = (bf16[3072,1024]{1,0:T(8,128)(2,1)}, f32[1024,768]{1,0:T(8,128)}, bf16[1024,768]{1,0:T(8,128)(2,1)}, f32[64,128]{1,0:T(8,128)}) custom-call(s32[38]{0:T(128)} %concatenate.84.info_ref.order_ref, bf16[1024,768]{1,0:T(8,128)(2,1)} %get-tuple-element.412.b_ref.refs_0_, bf16[1024,3072]{1,0:T(8,128)(2,1)} %get-tuple-element.391.refs_1_, ...), custom_call_target="tpu_custom_call" | custom-call | flops 900000000 | bytes 1800000 | tf_op jit(solution)/shard_map/ffn_back/pallas_call | solution.py:384
  179.6 7.2 %outer_keep.2 = (f32[768,768]{1,0:T(8,128)}, bf16[768,768]{1,0:T(8,128)(2,1)}) custom-call(bf16[3072,1024]{1,0:T(8,128)(2,1)} %get-tuple-element.411.a_ref, bf16[1024,768]{1,0:T(8,128)(2,1)} %get-tuple-element.412.b_ref.refs_0_, bf16[2,768,768]{2,1,0:T(8,128)(2,1)} %copy-done.22), custom_call_target="tpu_custom_call" | custom-call | flops 350000000 | bytes 700000 | tf_op jit(solution)/shard_map/outer_keep/pallas_call | solution.py:422
  186.8 5.9 %outer_send.3 = bf16[2,768,768]{2,1,0:T(8,128)(2,1)} custom-call(bf16[3072,1024]{1,0:T(8,128)(2,1)} %get-tuple-element.443.a_ref, bf16[1024,768]{1,0:T(8,128)(2,1)} %get-tuple-element.444.b_ref), custom_call_target="tpu_custom_call" | custom-call | flops 300000000 | bytes 600000 | tf_op jit(solution)/shard_map/outer_send/pallas_call | solution.py:400
  200.5 19.7 %attend_back.3 = (bf16[1024,384]{1,0:T(8,128)(2,1)}, bf16[1024,384]{1,0:T(8,128)(2,1)}, bf16[8,560,128]{2,1,0:T(8,128)(2,1)}, bf16[4,560,128]{2,1,0:T(8,128)(2,1...) custom-call(s32[38]{0:T(128)} %concatenate.84.info_ref.order_ref, ...), custom_call_target="tpu_custom_call" | custom-call | flops 1050000000 | bytes 2100000 | tf_op jit(solution)/shard_map/attend_back/pallas_call | solution.py:220
  226.9 7.2 %outer_keep.3 = (f32[768,768]{1,0:T(8,128)}, bf16[768,768]{1,0:T(8,128)(2,1)}) custom-call(bf16[3072,1024]{1,0:T(8,128)(2,1)} %get-tuple-element.443.a_ref, bf16[1024,768]{1,0:T(8,128)(2,1)} %get-tuple-element.444.b_ref, bf16[2,768,768]{2,1,0:T(8,128)(2,1)} %copy-done.21), custom_call_target="tpu_custom_call" | custom-call | flops 350000000 | bytes 700000 | tf_op jit(solution)/shard_map/outer_keep/pallas_call | solution.py:422
  240.5 17.5 %attend_back.4 = (bf16[1024,384]{1,0:T(8,128)(2,1)}, bf16[1024,384]{1,0:T(8,128)(2,1)}, bf16[8,416,128]{2,1,0:T(8,128)(2,1)}, bf16[4,416,128]{2,1,0:T(8,128)(2,1...) custom-call(s32[38]{0:T(128)} %concatenate.84.info_ref.order_ref, ...), custom_call_target="tpu_custom_call" | custom-call | flops 900000000 | bytes 1800000 | tf_op jit(solution)/shard_map/attend_back/pallas_call | solution.py:220
  266.1 17.6 %attend_back.5 = (bf16[1024,384]{1,0:T(8,128)(2,1)}, bf16[1024,384]{1,0:T(8,128)(2,1)}, bf16[8,416,128]{2,1,0:T(8,128)(2,1)}, bf16[4,416,128]{2,1,0:T(8,128)(2,1...) custom-call(s32[38]{0:T(128)} %concatenate.84.info_ref.order_ref, ...), custom_call_target="tpu_custom_call" | custom-call | flops 900000000 | bytes 1800000 | tf_op jit(solution)/shard_map/attend_back/pallas_call | solution.py:220
  297.5 10.4 %grad_tokens.1 = bf16[1024,768]{1,0:T(8,128)(2,1)} custom-call(s32[38]{0:T(128)} %concatenate.84.info_ref.order_ref, bf16[1024,384]{1,0:T(8,128)(2,1)} %get-tuple-element.500.refs_0_, bf16[1024,384]{1,0:T(8,128)(2,1)} %get-tuple-element.501.refs_1_, bf16[1024,384]{1,0:T(8,128)(2,1)} %get-tuple-element.502.refs_2_, bf16[1024,384]{1,0:T(8,128)(2,1)} %copy-done.37, ...), custom_call_target="tpu_custom_call" | custom-call | flops 450000000 | bytes 900000 | tf_op jit(solution)/shard_map/grad_tokens/pallas_call | solution.py:451
  308.7 5.1 %collective-permute-done.37 = bf16[8,416,128]{2,1,0:T(8,128)(2,1)S(1)} collective-permute-done((bf16[8,416,128]{2,1,0:T(8,128)(2,1)}, bf16[8,416,128]{2,1,0:T(8,128)(2,1)S(1)}, u32[]{:S(2)}, u32[]{:S(2)}) %collective-permute-start.37) | collective-permute-done | bytes 852000 | tf_op jit(solution)/shard_map/ppermute | solution.py:569
  328.6 5.9 %collective-permute-done.47 = bf16[96,768]{1,0:T(8,128)(2,1)S(1)} collective-permute-done((bf16[96,768]{1,0:T(8,128)(2,1)S(1)}, bf16[96,768]{1,0:T(8,128)(2,1)S(1)}, u32[]{:S(2)}, u32[]{:S(2)}) %collective-permute-start.47) | collective-permute-done | bytes 147488 | tf_op jit(solution)/shard_map/ppermute | solution.py:569
  334.6 5.2 %collective-permute-done.46 = bf16[2,416,128]{2,1,0:T(8,128)(2,1)S(1)} collective-permute-done((bf16[2,416,128]{2,1,0:T(8,128)(2,1)S(1)}, bf16[2,416,128]{2,1,0:T(8,128)(2,1)S(1)}, u32[]{:S(2)}, u32[]{:S(2)}) %collective-permute-start.46) | collective-permute-done | bytes 213024 | tf_op jit(solution)/shard_map/ppermute | solution.py:569
  349.7 8.3 %collective-permute-done.52 = bf16[2,96,768]{2,1,0:T(8,128)(2,1)S(1)} collective-permute-done((bf16[2,96,768]{2,1,0:T(8,128)(2,1)S(1)}, bf16[2,96,768]{2,1,0:T(8,128)(2,1)S(1)}, u32[]{:S(2)}, u32[]{:S(2)}) %collective-permute-start.52) | collective-permute-done | bytes 294944 | tf_op jit(solution)/shard_map/ppermute | solution.py:569
  374.4 4.9 %collective-permute-done.60 = bf16[4,304,128]{2,1,0:T(8,128)(2,1)S(1)} collective-permute-done((bf16[4,304,128]{2,1,0:T(8,128)(2,1)S(1)}, bf16[4,304,128]{2,1,0:T(8,128)(2,1)S(1)}, u32[]{:S(2)}, u32[]{:S(2)}) %collective-permute-start.60) | collective-permute-done | bytes 311328 | tf_op jit(solution)/shard_map/ppermute | solution.py:569
  384.6 6.4 %collective-permute-done.65 = bf16[2,2,96,768]{3,2,0,1:T(8,128)(2,1)S(1)} collective-permute-done((bf16[2,2,96,768]{3,2,0,1:T(8,128)(2,1)S(1)}, bf16[2,2,96,768]{3,2,0,1:T(8,128)(2,1)S(1)}, u32[]{:S(2)}, u32[]{:S(2)}) %collective-permute-start.65) | collective-permute-done | bytes 589856 | tf_op jit(solution)/shard_map/ppermute | solution.py:569
  397.2 7.1 %collective-permute-done.67 = bf16[8,160,128]{2,1,0:T(8,128)(2,1)S(1)} collective-permute-done((bf16[8,160,128]{2,1,0:T(8,128)(2,1)S(1)}, bf16[8,160,128]{2,1,0:T(8,128)(2,1)S(1)}, u32[]{:S(2)}, u32[]{:S(2)}) %collective-permute-start.67) | collective-permute-done | bytes 327712 | tf_op jit(solution)/shard_map/ppermute | solution.py:569
  405.5 5.6 %collective-permute-done.66 = bf16[8,160,128]{2,1,0:T(8,128)(2,1)S(1)} collective-permute-done((bf16[8,160,128]{2,1,0:T(8,128)(2,1)S(1)}, bf16[8,160,128]{2,1,0:T(8,128)(2,1)S(1)}, u32[]{:S(2)}, u32[]{:S(2)}) %collective-permute-start.66) | collective-permute-done | bytes 327712 | tf_op jit(solution)/shard_map/ppermute | solution.py:569
  417.0 5.0 %place_pair.3 = (f32[768,2304]{1,0:T(8,128)}, f32[256,128]{1,0:T(8,128)}, f32[256,128]{1,0:T(8,128)}) custom-call(s32[38]{0:T(128)} %concatenate.84.info_ref.order_ref, bf16[16,304,128]{2,1,0:T(8,128)(2,1)} %copy-done.5, bf16[16,304,128]{2,1,0:T(8,128)(2,1)} %copy-done.10), custom_call_target="tpu_custom_call" | custom-call | flops 150000000 | bytes 300000 | tf_op jit(solution)/shard_map/place_pair/pallas_call | solution.py:487
  423.7 4.7 %place_pair.4 = (f32[768,2304]{1,0:T(8,128)}, f32[256,128]{1,0:T(8,128)}, f32[256,128]{1,0:T(8,128)}) custom-call(s32[38]{0:T(128)} %concatenate.84.info_ref.order_ref, f32[768,2304]{1,0:T(8,128)} %get-tuple-element.590.refs_0_, bf16[16,160,128]{2,1,0:T(8,128)(2,1)} %copy-done.29, bf16[16,160,128]{2,1,0:T(8,128)(2,1)} %copy-done.40), custom_call_target="tpu_custom_call", output_to_operand_aliasing={{0}: (1, {})} | custom-call | flops 150000000 | bytes 300000 | tf_op jit(solution)/shard_map/place_pair/pallas_call | solution.py:487
  431.2 4.7 %place_pair.5 = (f32[768,2304]{1,0:T(8,128)}, f32[256,128]{1,0:T(8,128)}, f32[256,128]{1,0:T(8,128)}) custom-call(s32[38]{0:T(128)} %concatenate.84.info_ref.order_ref, f32[768,2304]{1,0:T(8,128)} %get-tuple-element.594.refs_0_, bf16[16,160,128]{2,1,0:T(8,128)(2,1)} %copy-done.30, bf16[16,160,128]{2,1,0:T(8,128)(2,1)} %copy-done.39), custom_call_target="tpu_custom_call", output_to_operand_aliasing={{0}: (1, {})} | custom-call | flops 150000000 | bytes 300000 | tf_op jit(solution)/shard_map/place_pair/pallas_call | solution.py:487
  (450 shorter events, 195.5 us)
Async XLA Ops:
  35.9 20.9 %collective-permute-start.10 = (bf16[4,2,32,512]{3,2,0,1:T(8,128)(2,1)S(1)}, bf16[4,2,32,512]{3,2,0,1:T(8,128)(2,1)S(1)}, u32[]{:S(2)}, u32[]{:S(2)}) collective-permute-start(bf16[4,2,32,512]{3,2,0,1:T(8,128)(2,1)S(1)} %pad_maximum_fusion.5), channel_id=1, source_target_pairs={{0,2},{1,3},{2,0},{3,1},{4,6},{5,7},{6,4},{7,5},{8,10},{9,11},{10,... | collective-permute-start | bytes 786440 | tf_op jit(solution)/shard_map/ppermute | solution.py:569
  62.4 20.6 %collective-permute-start.11 = (bf16[8,2,32,512]{3,2,0,1:T(8,128)(2,1)}, bf16[8,2,32,512]{3,2,0,1:T(8,128)(2,1)S(1)}, u32[]{:S(2)}, u32[]{:S(2)}) collective-permute-start(bf16[8,2,32,512]{3,2,0,1:T(8,128)(2,1)} %constant_dynamic-update-slice_fusion.2), channel_id=1, source_target_pairs={{0,2},{1,3},{2,0},{3,1},{4,6},{5,7},{6,4},{7,5},{8,10},{9,11},{10,... | collective-permute-start | bytes 1572872 | tf_op jit(solution)/shard_map/ppermute | solution.py:569
  71.9 32.9 %collective-permute-start.20 = (bf16[4,96,768]{2,1,0:T(8,128)(2,1)}, bf16[4,96,768]{2,1,0:T(8,128)(2,1)}, u32[]{:S(2)}, u32[]{:S(2)}) collective-permute-start(bf16[4,96,768]{2,1,0:T(8,128)(2,1)} %bitcast.34), channel_id=1, source_target_pairs={{0,4},{1,5},{2,6},{3,7},{4,0},{5,1},{6,2},{7,3},{8,12},{9,13},{10,... | collective-permute-start | bytes 1769480 | tf_op jit(solution)/shard_map/ppermute | solution.py:569
  73.5 44.3 %collective-permute-start.19 = (bf16[768,768]{1,0:T(8,128)(2,1)}, bf16[768,768]{1,0:T(8,128)(2,1)}, u32[]{:S(2)}, u32[]{:S(2)}) collective-permute-start(bf16[768,768]{1,0:T(8,128)(2,1)} %refs_7_), channel_id=1, source_target_pairs={{0,1},{1,0},{2,3},{3,2},{4,5},{5,4},{6,7},{7,6},{8,9},{9,8},{10,11... | collective-permute-start | bytes 3538952 | tf_op jit(solution)/shard_map/ppermute | solution.py:569
  77.5 40.3 %collective-permute-start.22 = (bf16[768,768]{1,0:T(8,128)(2,1)S(1)}, bf16[768,768]{1,0:T(8,128)(2,1)}, u32[]{:S(2)}, u32[]{:S(2)}) collective-permute-start(bf16[768,768]{1,0:T(8,128)(2,1)S(1)} %copy-done.4), channel_id=1, source_target_pairs={{0,1},{1,0},{2,3},{3,2},{4,5},{5,4},{6,7},{7,6},{8,9},{9,8},{10,11... | collective-permute-start | bytes 3538952 | tf_op jit(solution)/shard_map/ppermute | solution.py:569
  79.0 38.8 %collective-permute-start.23 = (bf16[768,768]{1,0:T(8,128)(2,1)S(1)}, bf16[768,768]{1,0:T(8,128)(2,1)}, u32[]{:S(2)}, u32[]{:S(2)}) collective-permute-start(bf16[768,768]{1,0:T(8,128)(2,1)S(1)} %bitcast.157), channel_id=1, source_target_pairs={{0,1},{1,0},{2,3},{3,2},{4,5},{5,4},{6,7},{7,6},{8,9},{9,8},{10,11... | collective-permute-start | bytes 3538952 | tf_op jit(solution)/shard_map/ppermute | solution.py:569
  157.4 20.8 %collective-permute-start.25 = (bf16[2,768,768]{2,1,0:T(8,128)(2,1)}, bf16[2,768,768]{2,1,0:T(8,128)(2,1)S(1)}, u32[]{:S(2)}, u32[]{:S(2)}) collective-permute-start(bf16[2,768,768]{2,1,0:T(8,128)(2,1)} %outer_send.2), channel_id=1, source_target_pairs={{0,1},{1,0},{2,3},{3,2},{4,5},{5,4},{6,7},{7,6},{8,9},{9,8},{10,11... | collective-permute-start | bytes 7077896 | tf_op jit(solution)/shard_map/ppermute | solution.py:569
  192.6 32.9 %collective-permute-start.29 = (bf16[2,768,768]{2,1,0:T(8,128)(2,1)}, bf16[2,768,768]{2,1,0:T(8,128)(2,1)S(1)}, u32[]{:S(2)}, u32[]{:S(2)}) collective-permute-start(bf16[2,768,768]{2,1,0:T(8,128)(2,1)} %outer_send.3), channel_id=1, source_target_pairs={{0,1},{1,0},{2,3},{3,2},{4,5},{5,4},{6,7},{7,6},{8,9},{9,8},{10,11... | collective-permute-start | bytes 7077896 | tf_op jit(solution)/shard_map/ppermute | solution.py:569
  193.0 28.3 %collective-permute-start.27 = (bf16[768,768]{1,0:T(8,128)(2,1)}, bf16[768,768]{1,0:T(8,128)(2,1)}, u32[]{:S(2)}, u32[]{:S(2)}) collective-permute-start(bf16[768,768]{1,0:T(8,128)(2,1)} %get-tuple-element.414), channel_id=1, source_target_pairs={{0,2},{1,3},{2,0},{3,1},{4,6},{5,7},{6,4},{7,5},{8,10},{9,11},{10,... | collective-permute-start | bytes 3538952 | tf_op jit(solution)/shard_map/ppermute | solution.py:569
  220.2 42.6 %collective-permute-start.26 = (bf16[8,560,128]{2,1,0:T(8,128)(2,1)}, bf16[8,560,128]{2,1,0:T(8,128)(2,1)}, u32[]{:S(2)}, u32[]{:S(2)}) collective-permute-start(bf16[8,560,128]{2,1,0:T(8,128)(2,1)} %get-tuple-element.438), channel_id=1, source_target_pairs={{0,4},{1,5},{2,6},{3,7},{4,0},{5,1},{6,2},{7,3},{8,12},{9,13},{10,... | collective-permute-start | bytes 3440648 | tf_op jit(solution)/shard_map/ppermute | solution.py:569
  223.7 36.5 %collective-permute-start.28 = (bf16[2,2,96,768]{3,2,0,1:T(8,128)(2,1)}, bf16[2,2,96,768]{3,2,0,1:T(8,128)(2,1)}, u32[]{:S(2)}, u32[]{:S(2)}) collective-permute-start(bf16[2,2,96,768]{3,2,0,1:T(8,128)(2,1)} %fusion.3), channel_id=1, source_target_pairs={{0,4},{1,5},{2,6},{3,7},{4,0},{5,1},{6,2},{7,3},{8,12},{9,13},{10,... | collective-permute-start | bytes 1769480 | tf_op jit(solution)/shard_map/ppermute | solution.py:569
  234.1 49.6 %collective-permute-start.36 = (bf16[768,768]{1,0:T(8,128)(2,1)}, bf16[768,768]{1,0:T(8,128)(2,1)}, u32[]{:S(2)}, u32[]{:S(2)}) collective-permute-start(bf16[768,768]{1,0:T(8,128)(2,1)} %get-tuple-element.446), channel_id=1, source_target_pairs={{0,2},{1,3},{2,0},{3,1},{4,6},{5,7},{6,4},{7,5},{8,10},{9,11},{10,... | collective-permute-start | bytes 3538952 | tf_op jit(solution)/shard_map/ppermute | solution.py:569
  234.7 59.7 %collective-permute-start.31 = (bf16[1024,384]{1,0:T(8,128)(2,1)}, bf16[1024,384]{1,0:T(8,128)(2,1)}, u32[]{:S(2)}, u32[]{:S(2)}) collective-permute-start(bf16[1024,384]{1,0:T(8,128)(2,1)} %get-tuple-element.484), channel_id=1, source_target_pairs={{0,1},{1,0},{2,3},{3,2},{4,5},{5,4},{6,7},{7,6},{8,9},{9,8},{10,11... | collective-permute-start | bytes 2359304 | tf_op jit(solution)/shard_map/ppermute | solution.py:569
  262.2 24.2 %collective-permute-start.35 = (bf16[2,96,768]{2,1,0:T(8,128)(2,1)}, bf16[2,96,768]{2,1,0:T(8,128)(2,1)}, u32[]{:S(2)}, u32[]{:S(2)}) collective-permute-start(bf16[2,96,768]{2,1,0:T(8,128)(2,1)} %fusion.6), channel_id=1, source_target_pairs={{0,8},{1,9},{2,10},{3,11},{4,12},{5,13},{6,14},{7,15},{8,0},{9,1},... | collective-permute-start | bytes 884744 | tf_op jit(solution)/shard_map/ppermute | solution.py:569
  264.0 25.7 %collective-permute-start.34 = (bf16[4,560,128]{2,1,0:T(8,128)(2,1)S(1)}, bf16[4,560,128]{2,1,0:T(8,128)(2,1)S(1)}, u32[]{:S(2)}, u32[]{:S(2)}) collective-permute-start(bf16[4,560,128]{2,1,0:T(8,128)(2,1)S(1)} %add_convert_fusion), channel_id=1, source_target_pairs={{0,2},{1,3},{2,0},{3,1},{4,6},{5,7},{6,4},{7,5},{8,10},{9,11},{10,... | collective-permute-start | bytes 1720328 | tf_op jit(solution)/shard_map/ppermute | solution.py:569
  264.3 27.4 %collective-permute-start.33 = (bf16[8,416,128]{2,1,0:T(8,128)(2,1)}, bf16[8,416,128]{2,1,0:T(8,128)(2,1)S(1)}, u32[]{:S(2)}, u32[]{:S(2)}) collective-permute-start(bf16[8,416,128]{2,1,0:T(8,128)(2,1)} %get-tuple-element.488), channel_id=1, source_target_pairs={{0,4},{1,5},{2,6},{3,7},{4,0},{5,1},{6,2},{7,3},{8,12},{9,13},{10,... | collective-permute-start | bytes 2555912 | tf_op jit(solution)/shard_map/ppermute | solution.py:569
  291.8 22.0 %collective-permute-start.37 = (bf16[8,416,128]{2,1,0:T(8,128)(2,1)}, bf16[8,416,128]{2,1,0:T(8,128)(2,1)S(1)}, u32[]{:S(2)}, u32[]{:S(2)}) collective-permute-start(bf16[8,416,128]{2,1,0:T(8,128)(2,1)} %get-tuple-element.509), channel_id=1, source_target_pairs={{0,2},{1,3},{2,0},{3,1},{4,6},{5,7},{6,4},{7,5},{8,10},{9,11},{10,... | collective-permute-start | bytes 2555912 | tf_op jit(solution)/shard_map/ppermute | solution.py:569
  294.4 21.4 %collective-permute-start.43 = (bf16[2,560,128]{2,1,0:T(8,128)(2,1)}, bf16[2,560,128]{2,1,0:T(8,128)(2,1)}, u32[]{:S(2)}, u32[]{:S(2)}) collective-permute-start(bf16[2,560,128]{2,1,0:T(8,128)(2,1)} %add_convert_fusion.3), channel_id=1, source_target_pairs={{0,8},{1,9},{2,10},{3,11},{4,12},{5,13},{6,14},{7,15},{8,0},{9,1},... | collective-permute-start | bytes 860168 | tf_op jit(solution)/shard_map/ppermute | solution.py:569
  295.9 21.8 %collective-permute-start.42 = (bf16[96,768]{1,0:T(8,128)(2,1)}, bf16[96,768]{1,0:T(8,128)(2,1)}, u32[]{:S(2)}, u32[]{:S(2)}) collective-permute-start(bf16[96,768]{1,0:T(8,128)(2,1)} %fusion.8), channel_id=1, source_target_pairs={{0,16},{1,17},{2,18},{3,19},{4,20},{5,21},{6,22},{7,23},{8,24},{9,... | collective-permute-start | bytes 442376 | tf_op jit(solution)/shard_map/ppermute | solution.py:569
  296.7 25.2 %collective-permute-start.41 = (bf16[4,416,128]{2,1,0:T(8,128)(2,1)}, bf16[4,416,128]{2,1,0:T(8,128)(2,1)}, u32[]{:S(2)}, u32[]{:S(2)}) collective-permute-start(bf16[4,416,128]{2,1,0:T(8,128)(2,1)} %add_convert_fusion.2), channel_id=1, source_target_pairs={{0,2},{1,3},{2,0},{3,1},{4,6},{5,7},{6,4},{7,5},{8,10},{9,11},{10,... | collective-permute-start | bytes 1277960 | tf_op jit(solution)/shard_map/ppermute | solution.py:569
  325.7 22.2 %collective-permute-start.44 = (bf16[2,416,128]{2,1,0:T(8,128)(2,1)S(1)}, bf16[2,416,128]{2,1,0:T(8,128)(2,1)S(1)}, u32[]{:S(2)}, u32[]{:S(2)}) collective-permute-start(bf16[2,416,128]{2,1,0:T(8,128)(2,1)S(1)} %add_convert_fusion.4), channel_id=1, source_target_pairs={{0,8},{1,9},{2,10},{3,11},{4,12},{5,13},{6,14},{7,15},{8,0},{9,1},... | collective-permute-start | bytes 638984 | tf_op jit(solution)/shard_map/ppermute | solution.py:569
  328.5 19.5 %collective-permute-start.53 = (bf16[1,304,128]{2,1,0:T(8,128)(2,1)S(1)}, bf16[1,304,128]{2,1,0:T(8,128)(2,1)S(1)}, u32[]{:S(2)}, u32[]{:S(2)}) collective-permute-start(bf16[1,304,128]{2,1,0:T(8,128)(2,1)S(1)} %fusion.13), channel_id=1, source_target_pairs={{0,16},{1,17},{2,18},{3,19},{4,20},{5,21},{6,22},{7,23},{8,24},{9,... | collective-permute-start | bytes 233480 | tf_op jit(solution)/shard_map/ppermute | solution.py:569
  334.6 23.5 %collective-permute-start.52 = (bf16[2,96,768]{2,1,0:T(8,128)(2,1)S(1)}, bf16[2,96,768]{2,1,0:T(8,128)(2,1)S(1)}, u32[]{:S(2)}, u32[]{:S(2)}) collective-permute-start(bf16[2,96,768]{2,1,0:T(8,128)(2,1)S(1)} %maximum_select_fusion.9), channel_id=1, source_target_pairs={{0,8},{1,9},{2,10},{3,11},{4,12},{5,13},{6,14},{7,15},{8,0},{9,1},... | collective-permute-start | bytes 884744 | tf_op jit(solution)/shard_map/ppermute | solution.py:569
  369.3 21.6 %collective-permute-start.65 = (bf16[2,2,96,768]{3,2,0,1:T(8,128)(2,1)S(1)}, bf16[2,2,96,768]{3,2,0,1:T(8,128)(2,1)S(1)}, u32[]{:S(2)}, u32[]{:S(2)}) collective-permute-start(bf16[2,2,96,768]{3,2,0,1:T(8,128)(2,1)S(1)} %maximum_select_fusion.7), channel_id=1, source_target_pairs={{0,4},{1,5},{2,6},{3,7},{4,0},{5,1},{6,2},{7,3},{8,12},{9,13},{10,... | collective-permute-start | bytes 1769480 | tf_op jit(solution)/shard_map/ppermute | solution.py:569
  (113 other events, 1041.7 us)
